TPU v7x, 32 devices: a whole 2x2x4 slice. The times are simulated.
32 devices in a mesh: dp: 8 (over z, y), mp: 4 (over x, core).
Axes of the slice: x: 2, y: 2, z: 4, core: 2. Of those that a mesh axis runs over, the one named last changes fastest.
Arguments:
- tokens: bfloat16 [16384, 768], P('dp'), may hold values from -6 to 6
- cotangent: bfloat16 [16384, 768], P('dp'), may hold values from -6 to 6
- seq_lengths: int32 [32], replicated, may hold values from 1 to 768, as said below
- seq_bin: int32 [32], replicated, may hold values from 0 to 15, as said below
- qkv_weight: bfloat16 [3, 768, 768], P(None, 'dp', 'mp'), may hold values from -0.21875 to 0.21875
- out_weight: bfloat16 [768, 768], P('mp', 'dp'), may hold values from -0.875 to 0.875
- up_weight: bfloat16 [768, 3072], P('dp', 'mp'), may hold values from -0.21875 to 0.21875
- down_weight: bfloat16 [3072, 768], P('mp', 'dp'), may hold values from -0.109375 to 0.109375
- norm_gains: float32 [2, 768], replicated, may hold values from 0.5 to 1.5
- shared_biases: float32 [4, 768], replicated, may hold values from -1.8 to 1.8
- head_biases: float32 [2, 768], P(None, 'mp'), may hold values from -1.8 to 1.8
- unit_bias: float32 [3072], P('mp'), may hold values from -0.6 to 0.6
- qkv_moment: float32 [3, 768, 768], P(None, 'dp', 'mp'), may hold values from -768 to 768
- out_moment: float32 [768, 768], P('mp', 'dp'), may hold values from -192 to 192
- up_moment: float32 [768, 3072], P('dp', 'mp'), may hold values from -128 to 128
- down_moment: float32 [3072, 768], P('mp', 'dp'), may hold values from -320 to 320
- gain_moment: float32 [2, 768], replicated, may hold values from -640 to 640
- bias_moment: float32 [4, 768], replicated, may hold values from -640 to 640
- head_moment: float32 [2, 768], P(None, 'mp'), may hold values from -640 to 640
- unit_moment: float32 [3072], P('mp'), may hold values from -128 to 128
Outputs:
- block_out: float32 [16384, 768], P('dp')
- input_grad: float32 [16384, 768], P('dp')
- qkv_moment_next: float32 [3, 768, 768], P(None, 'dp', 'mp')
- qkv_next: float32 [3, 768, 768], P(None, 'dp', 'mp')
- out_moment_next: float32 [768, 768], P('mp', 'dp')
- out_next: float32 [768, 768], P('mp', 'dp')
- up_moment_next: float32 [768, 3072], P('dp', 'mp')
- up_next: float32 [768, 3072], P('dp', 'mp')
- down_moment_next: float32 [3072, 768], P('mp', 'dp')
- down_next: float32 [3072, 768], P('mp', 'dp')
- gain_moment_next: float32 [2, 768], replicated
- gain_next: float32 [2, 768], replicated
- bias_moment_next: float32 [4, 768], replicated
- bias_next: float32 [4, 768], replicated
- head_moment_next: float32 [2, 768], P(None, 'mp')
- head_next: float32 [2, 768], P(None, 'mp')
- unit_moment_next: float32 [3072], P('mp')
- unit_next: float32 [3072], P('mp')
Inputs may be any that keep to these rules, and one draw needn't show every extreme that they name: `seq_lengths`: one sequence is exactly 768 long. Sequence s lies in bin seq_bin[s]; bin b (rows b * 1024 to (b + 1) * 1024 - 1 of tokens, on index b // 2 of dp) holds exactly two sequences, packed from its first row in the order of their indices; their lengths add up to 1024 or less, and the rows after them are unused.
All inputs are finite; a program needn't handle non-finite values.
Results may differ from a plain program's by a relative error of at most 0.024.
Values may be sent and summed in bfloat16 or wider, within the bound.
No kernel may reach another device: no remote copies, remote signals or barrier semaphores. Data moves between devices by JAX's collectives and lax.ppermute only.
A program may use at most 192 MiB of HBM per device.

v0:
```python
import math

import jax
import jax.numpy as jnp
from jax import lax
from jax.sharding import PartitionSpec as P

D = 768
HEAD_DIM = 64
FF = 3072
SLOTS = 1024
MICRO = 2
NS_STEPS = 5


EPS = 1e-05
MOMENTUM = 0.9
NS_A = 3.4445
NS_B = -4.775
NS_C = 2.0315
RATE = 1.0
DECAY = 0.01
VECTOR_RATE = 0.1
FLOOR = -1e30


def in_blocks(shard, dim, length):
    before, after = (shard.shape[:dim], shard.shape[dim + 1 :])
    return jnp.moveaxis(shard.reshape(*before, length, -1, *after), dim, 0)


def summed_on_arrival(shard, axis, dim):
    blocks = in_blocks(shard, dim, lax.axis_size(axis))
    arrived = lax.all_to_all(blocks, axis, split_axis=0, concat_axis=0, tiled=True)
    return arrived.astype(jnp.float32).sum(axis=0)


def as_sent(shard):
    return jax.tree.map(lambda a: a.astype(jnp.bfloat16) if a.dtype == jnp.float32 else a, shard)


def highest(left, right):
    return jnp.dot(left, right, precision=lax.Precision.HIGHEST, preferred_element_type=jnp.float32)


def layer_norm(rows, gain, shift):
    centre = rows - jnp.mean(rows, axis=-1, keepdims=True)
    spread = jnp.mean(centre * centre, axis=-1, keepdims=True)
    return centre * lax.rsqrt(spread + EPS) * gain + shift


def segments_of(seq_lengths, seq_bin, index):
    count = seq_lengths.shape[0]
    order = jnp.arange(count, dtype=jnp.int32)
    inside = seq_bin == index
    leader = jnp.min(jnp.where(inside, order, count))
    first = jnp.sum(jnp.where(order == leader, seq_lengths, 0))
    total = jnp.sum(jnp.where(inside, seq_lengths, 0))
    slot = jnp.arange(SLOTS, dtype=jnp.int32)
    segment = jnp.where(slot < first, 0, jnp.where(slot < total, 1, slot + 2))
    return (segment, slot < total)


def causal_mask(segment):
    order = jnp.arange(segment.shape[0], dtype=jnp.int32)
    return (segment[:, None] == segment[None, :]) & (order[None, :] <= order[:, None])


def split_heads(block):
    return block.reshape(block.shape[0], block.shape[1] // HEAD_DIM, HEAD_DIM)


def attend(query, keys, values, causal):
    scores = jnp.einsum(
        "qhd,khd->hqk", split_heads(query), split_heads(keys), preferred_element_type=jnp.float32
    )
    scores = jnp.where(causal[None], scores, FLOOR)
    top = jnp.max(scores, axis=-1, keepdims=True)
    raised = jnp.exp(scores - top)
    total = jnp.sum(raised, axis=-1, keepdims=True)
    weights = (raised / total).astype(jnp.bfloat16)
    mixed = jnp.einsum(
        "hqk,khd->qhd", weights, split_heads(values), preferred_element_type=jnp.float32
    )
    return (mixed.reshape(query.shape), top + jnp.log(total))


def attend_back(query, keys, values, log_total, causal, grad_mixed):
    heads_query = split_heads(query)
    heads_keys = split_heads(keys)
    heads_values = split_heads(values)
    grad_heads = split_heads(grad_mixed)
    scores = jnp.einsum("qhd,khd->hqk", heads_query, heads_keys, preferred_element_type=jnp.float32)
    weights = jnp.where(causal[None], jnp.exp(scores - log_total), 0.0)
    grad_values = jnp.einsum(
        "hqk,qhd->khd", weights.astype(jnp.bfloat16), grad_heads, preferred_element_type=jnp.float32
    )
    grad_weights = jnp.einsum(
        "qhd,khd->hqk", grad_heads, heads_values, preferred_element_type=jnp.float32
    )
    inner = jnp.sum(weights * grad_weights, axis=-1, keepdims=True)
    grad_scores = (weights * (grad_weights - inner)).astype(jnp.bfloat16)
    grad_query = jnp.einsum(
        "hqk,khd->qhd", grad_scores, heads_keys, preferred_element_type=jnp.float32
    )
    grad_keys = jnp.einsum(
        "hqk,qhd->khd", grad_scores, heads_query, preferred_element_type=jnp.float32
    )
    shape = query.shape
    return (
        grad_query.reshape(shape).astype(jnp.bfloat16),
        grad_keys.reshape(shape).astype(jnp.bfloat16),
        grad_values.reshape(shape).astype(jnp.bfloat16),
    )


def newton(panel):
    current = panel
    for step in range(NS_STEPS):
        gram = lax.psum(highest(current, current.T).astype(jnp.bfloat16), "mp").astype(jnp.float32)
        if step == 0:
            factor = 1.0 / (jnp.sqrt(jnp.trace(gram)) + 1e-07)
            current = current * factor
            gram = gram * (factor * factor)
        poly = NS_B * gram + NS_C * highest(gram, gram)
        current = NS_A * current + highest(poly, current)
    return current


def on_device(
    tokens,
    cotangent,
    seq_lengths,
    seq_bin,
    qkv_weight,
    out_weight,
    up_weight,
    down_weight,
    norm_gains,
    shared_biases,
    head_biases,
    unit_bias,
    qkv_moment,
    out_moment,
    up_moment,
    down_moment,
    gain_moment,
    bias_moment,
    head_moment,
    unit_moment,
):
    position = lax.axis_index("dp")
    groups = lax.axis_size("dp")
    rows_each = qkv_weight.shape[1]
    scale = HEAD_DIM ** (-0.5)

    def fetch():
        return (
            lax.all_gather(qkv_weight, "dp", axis=1, tiled=True),
            lax.all_gather(out_weight, "dp", axis=1, tiled=True),
            lax.all_gather(up_weight, "dp", axis=0, tiled=True),
            lax.all_gather(down_weight, "dp", axis=1, tiled=True),
        )

    def across_heads(partial_value):
        return lax.psum(partial_value.astype(jnp.bfloat16), "mp").astype(jnp.float32)

    outputs = []
    input_grads = []
    local = None
    reduced = None
    vectors = None
    for block in range(MICRO):
        start = block * SLOTS
        rows = tokens[start : start + SLOTS]
        segment, valid = segments_of(seq_lengths, seq_bin, position * MICRO + block)
        causal = causal_mask(segment)
        matrices = fetch()
        forward_qkv_full, forward_out_full, forward_up_full, forward_down_full = matrices
        forward_source = rows.astype(jnp.float32)
        forward_normed = layer_norm(forward_source, norm_gains[0], shared_biases[0]).astype(
            jnp.bfloat16
        )
        project = jnp.einsum(
            "rd,tdc->rtc", forward_normed, forward_qkv_full, preferred_element_type=jnp.float32
        )
        forward_query = ((project[:, 0] + head_biases[0]) * scale).astype(jnp.bfloat16)
        forward_keys = project[:, 1].astype(jnp.bfloat16)
        forward_values = (project[:, 2] + head_biases[1]).astype(jnp.bfloat16)
        forward_mixed, forward_log_total = attend(
            forward_query, forward_keys, forward_values, causal
        )
        forward_mixed = forward_mixed.astype(jnp.bfloat16)
        forward_hidden = forward_source + (
            across_heads(
                jnp.dot(forward_mixed, forward_out_full, preferred_element_type=jnp.float32)
            )
            + shared_biases[2]
        )
        forward_normed_two = layer_norm(forward_hidden, norm_gains[1], shared_biases[1]).astype(
            jnp.bfloat16
        )
        forward_before = (
            jnp.dot(forward_normed_two, forward_up_full, preferred_element_type=jnp.float32)
            + unit_bias
        )
        forward_active = jax.nn.gelu(forward_before).astype(jnp.bfloat16)
        result = forward_hidden + (
            across_heads(
                jnp.dot(forward_active, forward_down_full, preferred_element_type=jnp.float32)
            )
            + shared_biases[3]
        )
        forward_kept = (
            forward_source,
            forward_normed,
            forward_query,
            forward_keys,
            forward_values,
            forward_log_total,
            forward_mixed,
            forward_hidden,
            forward_normed_two,
            forward_before,
            forward_active,
        )
        result, kept = (result, forward_kept)
        matrices = fetch()
        grad_rows = cotangent[start : start + SLOTS] * valid[:, None].astype(jnp.bfloat16)
        qkv_full, out_full, up_full, down_full = matrices
        (
            source,
            normed,
            query,
            keys,
            values,
            log_total,
            mixed,
            hidden,
            normed_two,
            before,
            active,
        ) = kept
        grad_result = grad_rows.astype(jnp.float32)
        grad_down = jnp.einsum("ru,rd->ud", active, grad_rows, preferred_element_type=jnp.float32)
        grad_active = jnp.einsum(
            "rd,ud->ru", grad_rows, down_full, preferred_element_type=jnp.float32
        )
        grad_before = jax.vjp(jax.nn.gelu, before)[1](grad_active)[0].astype(jnp.bfloat16)
        grad_up = jnp.einsum(
            "rd,ru->du", normed_two, grad_before, preferred_element_type=jnp.float32
        )
        grad_normed_two = across_heads(
            jnp.einsum("ru,du->rd", grad_before, up_full, preferred_element_type=jnp.float32)
        )
        grad_hidden, grad_gain_two, grad_shift_two = jax.vjp(
            layer_norm, hidden, norm_gains[1], shared_biases[1]
        )[1](grad_normed_two)
        grad_hidden = grad_hidden + grad_result
        grad_branch = grad_hidden.astype(jnp.bfloat16)
        grad_out = jnp.einsum("rc,rd->cd", mixed, grad_branch, preferred_element_type=jnp.float32)
        grad_mixed = jnp.einsum(
            "rd,cd->rc", grad_branch, out_full, preferred_element_type=jnp.float32
        ).astype(jnp.bfloat16)
        grad_query, grad_keys, grad_values = attend_back(
            query, keys, values, log_total, causal, grad_mixed
        )
        grad_query = (grad_query.astype(jnp.float32) * scale).astype(jnp.bfloat16)
        stacked = jnp.stack((grad_query, grad_keys, grad_values), axis=1)
        grad_qkv = jnp.einsum("rd,rtc->tdc", normed, stacked, preferred_element_type=jnp.float32)
        grad_normed = across_heads(
            jnp.einsum("rtc,tdc->rd", stacked, qkv_full, preferred_element_type=jnp.float32)
        )
        grad_source, grad_gain_one, grad_shift_one = jax.vjp(
            layer_norm, source, norm_gains[0], shared_biases[0]
        )[1](grad_normed)
        grad_input = grad_hidden + grad_source
        grad_gains = jnp.stack((grad_gain_one, grad_gain_two))
        grad_biases = jnp.stack(
            (
                grad_shift_one,
                grad_shift_two,
                jnp.sum(grad_branch.astype(jnp.float32), axis=0),
                jnp.sum(grad_result, axis=0),
            )
        )
        grad_heads = jnp.stack(
            (
                jnp.sum(grad_query.astype(jnp.float32), axis=0),
                jnp.sum(grad_values.astype(jnp.float32), axis=0),
            )
        )
        grad_units = jnp.sum(grad_before.astype(jnp.float32), axis=0)
        grad_input, grads, small = (
            grad_input,
            (grad_qkv, grad_out, grad_up, grad_down),
            (grad_gains, grad_biases, grad_heads, grad_units),
        )
        outputs.append(result)
        input_grads.append(grad_input)
        vectors = small if vectors is None else jax.tree.map(jnp.add, vectors, small)
        local = grads if local is None else jax.tree.map(jnp.add, local, grads)
    reduced = (
        summed_on_arrival(local[0].astype(jnp.bfloat16), "dp", 1),
        summed_on_arrival(local[1].astype(jnp.bfloat16), "dp", 1),
        summed_on_arrival(local[2].astype(jnp.bfloat16), "dp", 0),
        summed_on_arrival(local[3].astype(jnp.bfloat16), "dp", 1),
    )
    gains_sum, biases_sum, heads_sum, units_sum = lax.psum(vectors, "dp")
    moments = (qkv_moment, out_moment, up_moment, down_moment)
    next_moments = tuple((MOMENTUM * moment + grad for moment, grad in zip(moments, reduced)))
    nesterov = tuple((grad + MOMENTUM * moment for moment, grad in zip(next_moments, reduced)))
    spacing = groups // 6
    local_panels = (
        nesterov[0][0],
        nesterov[0][1],
        nesterov[0][2],
        nesterov[1].T,
        nesterov[2],
        nesterov[3].T,
    )
    width_all = nesterov[2].shape[1]
    outgoing = jnp.zeros((groups, rows_each, width_all), jnp.float32)
    for number in range(6):
        shard = local_panels[number]
        shard = jnp.pad(shard, ((0, 0), (0, width_all - shard.shape[1])))
        outgoing = outgoing.at[number * spacing].set(shard)
    incoming = lax.all_to_all(
        outgoing.astype(jnp.bfloat16), "dp", split_axis=0, concat_axis=0, tiled=True
    ).astype(outgoing.dtype)
    chosen = incoming.reshape(groups * rows_each, width_all)
    orth = newton(chosen)
    back = lax.all_to_all(
        as_sent(orth.reshape(groups, rows_each, width_all)),
        "dp",
        split_axis=0,
        concat_axis=0,
        tiled=True,
    )
    returned = [back[number * spacing][:, : local_panels[number].shape[1]] for number in range(6)]
    orth_qkv = jnp.stack(returned[:3])
    orth_out = returned[3].T
    orth_up = returned[4]
    orth_down = returned[5].T
    keep_share = 1.0 - RATE * DECAY
    up_factor = math.sqrt(max(1.0, FF / D))
    qkv_next = qkv_weight.astype(jnp.float32) * keep_share - RATE * orth_qkv
    out_next = out_weight.astype(jnp.float32) * keep_share - RATE * orth_out
    up_next = up_weight.astype(jnp.float32) * keep_share - RATE * up_factor * orth_up
    down_next = down_weight.astype(jnp.float32) * keep_share - RATE * orth_down
    rate_vector = VECTOR_RATE / math.sqrt(groups * tokens.shape[0])
    gain_moment_next = MOMENTUM * gain_moment + gains_sum
    bias_moment_next = MOMENTUM * bias_moment + biases_sum
    head_moment_next = MOMENTUM * head_moment + heads_sum
    unit_moment_next = MOMENTUM * unit_moment + units_sum
    gain_next = norm_gains - rate_vector * gain_moment_next
    bias_next = shared_biases - rate_vector * bias_moment_next
    head_next = head_biases - rate_vector * head_moment_next
    unit_next = unit_bias - rate_vector * unit_moment_next
    block_out = jnp.concatenate(outputs, axis=0)
    input_grad = jnp.concatenate(input_grads, axis=0)
    return (
        block_out,
        input_grad,
        next_moments[0],
        qkv_next,
        next_moments[1],
        out_next,
        next_moments[2],
        up_next,
        next_moments[3],
        down_next,
        gain_moment_next,
        gain_next,
        bias_moment_next,
        bias_next,
        head_moment_next,
        head_next,
        unit_moment_next,
        unit_next,
    )


def solution(mesh):
    in_specs = (
        P("dp", None),
        P("dp", None),
        P(),
        P(),
        P(None, "dp", "mp"),
        P("mp", "dp"),
        P("dp", "mp"),
        P("mp", "dp"),
        P(),
        P(),
        P(None, "mp"),
        P("mp"),
        P(None, "dp", "mp"),
        P("mp", "dp"),
        P("dp", "mp"),
        P("mp", "dp"),
        P(),
        P(),
        P(None, "mp"),
        P("mp"),
    )
    out_specs = (
        P("dp", None),
        P("dp", None),
        P(None, "dp", "mp"),
        P(None, "dp", "mp"),
        P("mp", "dp"),
        P("mp", "dp"),
        P("dp", "mp"),
        P("dp", "mp"),
        P("mp", "dp"),
        P("mp", "dp"),
        P(),
        P(),
        P(),
        P(),
        P(None, "mp"),
        P(None, "mp"),
        P("mp"),
        P("mp"),
    )
    return jax.shard_map(
        on_device, mesh=mesh, in_specs=in_specs, out_specs=out_specs, check_vma=False
    )
```

profile of v0, /device:TPU:0, one launch (start us, length us, event | category | flops | bytes accessed | tf_op | source)
XLA Modules:
  0.0 1038.9 jit_solution(2635782957479531668)
XLA Ops:
  13.9 40.3 %all_gather.8 = bf16[3,768,192]{2,0,1:T(4,128)(2,1)} all-gather(bf16[3,96,192]{2,0,1:T(4,128)(2,1)S(1)} %copy.158), channel_id=1, replica_groups=mesh['dp'=8,'mp'=4] {'dp'}, dimensions={1}, use_global_device_ids=true | all-gather | bytes 995328 | tf_op jit(solution)/shard_map/all_gather | solution.py:159
  67.6 31.4 %all_gather.9 = bf16[192,768]{0,1:T(8,128)(2,1)S(1)} all-gather(bf16[192,96]{0,1:T(8,128)(2,1)} %copy.161), channel_id=1, replica_groups=mesh['dp'=8,'mp'=4] {'dp'}, dimensions={1}, use_global_device_ids=true | all-gather | bytes 331776 | tf_op jit(solution)/shard_map/all_gather | solution.py:160
  102.8 8.4 select_reduce_fusion.1
  111.3 7.0 fusion
  118.3 6.5 fusion.125
  130.7 38.4 %all-reduce.17.cloned.1.call-done = bf16[1024,768]{1,0:T(8,128)(2,1)} async-done(((bf16[1024,768]{1,0:T(8,128)(2,1)}), bf16[1024,768]{1,0:T(8,128)(2,1)}) %all-reduce.17.cloned.1.call-update) | async-done | bytes 1572880 | tf_op jit(solution)/shard_map/psum | solution.py:166
  175.4 5.9 select_reduce_fusion
  181.3 6.9 fusion.1
  188.3 6.5 fusion.124
  203.6 36.9 %all-reduce.19.cloned.1.call-done = bf16[1024,768]{1,0:T(8,128)(2,1)} async-done(((bf16[1024,768]{1,0:T(8,128)(2,1)}), bf16[1024,768]{1,0:T(8,128)(2,1)}) %all-reduce.19.cloned.1.call-update) | async-done | bytes 1572880 | tf_op jit(solution)/shard_map/psum | solution.py:166
  245.9 5.5 fusion.181
  258.5 25.0 %all-gather.5.cloned.1.call-done = bf16[768,768]{0,1:T(8,128)(2,1)} async-done(((bf16[768,96]{0,1:T(8,128)(2,1)}), bf16[768,768]{0,1:T(8,128)(2,1)}) %all-gather.5.cloned.1.call-update) | async-done | bytes 1179664 | tf_op jit(solution)/shard_map/all_gather | solution.py:162
  283.5 6.5 convert_reduce_fusion.9
  299.6 6.2 add_convert_fusion.3
  317.5 49.4 %all-reduce.31.cloned.1.call-done = (bf16[1024,768]{1,0:T(8,128)(2,1)}, bf16[1024,768]{1,0:T(8,128)(2,1)}) async-done(((bf16[1024,768]{1,0:T(8,128)(2,1)}, bf16[1024,768]{1,0:T(8,128)(2,1)}), (bf16[1024,768]{1,0:T(8,128)(2,1)}, bf16[1024,768]{1,0:T(8,128)(2,1)})) %all-reduce.31.cloned.1.call-update) | async-done | bytes 3145744 | tf_op jit(solution)/shard_map/psum | solution.py:166
  366.9 5.8 fusion.35
  372.9 5.0 fusion.54
  390.8 13.3 %multiply_reduce_fusion.1 = (f32[3,1024]{1,0:T(4,128)S(1)}, f32[3,1024,1024]{1,2,0:T(8,128)}) fusion(f32[3,1024,1024]{1,2,0:T(8,128)} %get-tuple-element.285, f32[3,1024]{1,0:T(4,128)} %log_add_fusion.1, pred[1024,1024]{0,1:T(8,128)(4,1)} %copy-done.14, bf16[1024,3,64]{0,2,1:T(8,128)(2,1)} %bitcast.216, f32[1024,3,64]{0,2,1:T(8,128)} %bitcast.204, ...), kind=kOutput, calls=%fused_computation.4 | convolution fusion | flops 415626240 | bytes 27419392 | tf_op jit(solution)/shard_map/qhd,khd->hqk/dot_general | solution.py:98
  404.2 7.1 multiply_convert_fusion.1
  414.1 13.4 %multiply_reduce_fusion = (f32[3,1024]{1,0:T(4,128)S(1)}, f32[3,1024,1024]{1,2,0:T(8,128)}) fusion(f32[3,1024,1024]{1,2,0:T(8,128)} %get-tuple-element.287, f32[3,1024]{1,0:T(4,128)S(1)} %copy-done.70, pred[1024,1024]{0,1:T(8,128)(4,1)} %fusion.20, bf16[1024,3,64]{0,2,1:T(8,128)(2,1)} %bitcast.218, f32[1024,3,64]{0,2,1:T(8,128)} %bitcast.207, ...), kind=kOutput, calls=%fused_computation.1 | convolution fusion | flops 415626240 | bytes 27419392 | tf_op jit(solution)/shard_map/qhd,khd->hqk/dot_general | solution.py:98
  430.1 7.2 multiply_convert_fusion
  442.8 5.5 all-to-all-start.2
  448.4 5.5 convert_reduce_fusion.16
  453.9 7.5 convert_reduce_fusion.15
  465.4 11.5 %all-to-all-done.2 = bf16[8,96,768]{2,1,0:T(8,128)(2,1)} async-done(((bf16[8,96,768]{2,1,0:T(8,128)(2,1)}), bf16[8,96,768]{2,1,0:T(8,128)(2,1)}, u32[]{:S(2)}, u32[]{:S(2)}) %all-to-all-start.2) | async-done | bytes 1179680 | tf_op jit(solution)/shard_map/all_to_all | solution.py:34
  492.4 5.1 all-to-all-start
  506.8 19.2 %all-to-all-done = bf16[8,3,96,192]{2,3,1,0:T(8,128)(2,1)} async-done(((bf16[8,3,96,192]{2,3,1,0:T(8,128)(2,1)}), bf16[8,3,96,192]{2,3,1,0:T(8,128)(2,1)}, u32[]{:S(2)}, u32[]{:S(2)}) %all-to-all-start) | async-done | bytes 884768 | tf_op jit(solution)/shard_map/all_to_all | solution.py:34
  532.9 32.4 %all_to_all.30 = bf16[8,96,768]{2,1,0:T(8,128)(2,1)S(1)} all-to-all(bf16[8,96,768]{2,1,0:T(8,128)(2,1)S(1)} %get-tuple-element.261), channel_id=1, replica_groups=mesh['dp'=8,'mp'=4] {'dp'}, dimensions={0} | all-to-all | bytes 2359296 | tf_op jit(solution)/shard_map/all_to_all | solution.py:328
  568.5 35.5 %all-reduce.21.cloned.1.call-done = bf16[768,768]{1,0:T(8,128)(2,1)} async-done(((bf16[768,768]{1,0:T(8,128)(2,1)}), bf16[768,768]{1,0:T(8,128)(2,1)}) %all-reduce.21.cloned.1.call-update) | async-done | bytes 1179664 | tf_op jit(solution)/shard_map/psum | solution.py:120
  608.3 6.1 fusion.58
  614.4 6.3 multiply_add_fusion.3
  622.1 7.1 convolution_convert_fusion.9
  629.2 37.6 %all-reduce.23.cloned.1.call-done = bf16[768,768]{1,0:T(8,128)(2,1)} async-done(((bf16[768,768]{1,0:T(8,128)(2,1)}), bf16[768,768]{1,0:T(8,128)(2,1)}) %all-reduce.23.cloned.1.call-update) | async-done | bytes 1179664 | tf_op jit(solution)/shard_map/psum | solution.py:120
  669.8 6.2 multiply_add_fusion.2
  677.4 7.3 convolution_convert_fusion.8
  684.8 5.6 convolution_convert_fusion.2
  693.7 28.7 %all-reduce.25.cloned.1.call-done = bf16[768,768]{1,0:T(8,128)(2,1)} async-done(((bf16[768,768]{1,0:T(8,128)(2,1)}), bf16[768,768]{1,0:T(8,128)(2,1)}) %all-reduce.25.cloned.1.call-update) | async-done | bytes 1179664 | tf_op jit(solution)/shard_map/psum | solution.py:120
  725.3 6.2 multiply_add_fusion.1
  732.9 7.1 convolution_convert_fusion.7
  747.0 30.7 %all-reduce.27.cloned.1.call-done = bf16[768,768]{1,0:T(8,128)(2,1)} async-done(((bf16[768,768]{1,0:T(8,128)(2,1)}), bf16[768,768]{1,0:T(8,128)(2,1)}) %all-reduce.27.cloned.1.call-update) | async-done | bytes 1179664 | tf_op jit(solution)/shard_map/psum | solution.py:120
  780.6 6.2 multiply_add_fusion
  788.2 7.1 convolution_convert_fusion.6
  800.6 134.6 %all-reduce.29.cloned.1.call-done = (bf16[1024,768]{1,0:T(8,128)(2,1)}, bf16[1024,768]{1,0:T(8,128)(2,1)}, bf16[1024,768]{1,0:T(8,128)(2,1)}, bf16[1024,768]{1,0:T(8,128)(2,1)}, bf16[768,768]{1,0:T(8,128)(2,1)}) async-done(((bf16[1024,768]{1,0:T(8,128)(2,1)}, bf16[1024,768]{1,0:T(8,128)(2,1)}, bf16[1024,768]{1,0:T(8,128)(2,1)}, bf16[1024,768]{1,0:T(8,128)(2,1)}, bf16[768,768]{1,0:T(8,128)(2,1)}), ...) | async-done | bytes 7471120 | tf_op jit(solution)/shard_map/psum | solution.py:166
  940.6 7.1 add_convert_fusion.2
  947.8 5.8 all-to-all-start.5
  953.8 8.8 fusion.55
  962.8 42.3 %all-reduce.5 = (f32[2,768]{1,0:T(2,128)S(1)}, f32[4,768]{1,0:T(4,128)S(1)}, f32[2,192]{1,0:T(2,128)S(1)}, f32[768]{0:T(1024)S(1)}) all-reduce(f32[2,768]{1,0:T(2,128)S(1)} %maximum_add_fusion.1, f32[4,768]{1,0:T(4,128)S(1)} %maximum_add_fusion, f32[2,192]{1,0:T(2,128)S(1)} %copy-done.143, ...), channel_id=1, replica_groups=mesh['dp'=8,'mp'=4] {'dp'}, use_global_device_ids=true, to_apply=%region_50.51 | all-reduce | flops 5760 | bytes 46080 | tf_op jit(solution)/shard_map/psum | solution.py:309
  1006.5 5.8 add_add_fusion.5
  (539 shorter events, 198.6 us)
Async XLA Ops:
  8.0 161.0 %all-reduce.17.cloned.1.call-start = ((), (), s32[]{:S(2)}) async-start(), calls=%async_computation.6 | async-start | bytes 3145728 | tf_op jit(solution)/shard_map/psum | solution.py:166
  9.8 48.5 %copy-start.75 = (f32[1024]{0:T(1024)}, f32[1024]{0:T(1024)S(1)}, u32[]{:S(2)}) copy-start(f32[1024]{0:T(1024)S(1)} %broadcast_multiply_fusion.3) | copy-start | bytes 12292
  9.8 47.9 %copy-start.97 = (f32[4,768]{1,0:T(4,128)S(1)}, f32[4,768]{1,0:T(4,128)}, u32[]{:S(2)}) copy-start(f32[4,768]{1,0:T(4,128)} %param.41) | copy-start | bytes 36868
  9.8 47.9 %copy-start.119 = (f32[2,768]{1,0:T(2,128)S(1)}, f32[2,768]{1,0:T(2,128)}, u32[]{:S(2)}) copy-start(f32[2,768]{1,0:T(2,128)} %param.40) | copy-start | bytes 18436
  9.8 48.5 %copy-start = (bf16[2048,768]{1,0:T(8,128)(2,1)S(1)}, bf16[2048,768]{1,0:T(8,128)(2,1)}, u32[]{:S(2)}) copy-start(bf16[2048,768]{1,0:T(8,128)(2,1)} %param.32) | copy-start | bytes 9437188
  13.3 47.5 %copy-start.99 = (f32[1024]{0:T(1024)}, f32[1024]{0:T(1024)S(1)}, u32[]{:S(2)}) copy-start(f32[1024]{0:T(1024)S(1)} %fusion.147) | copy-start | bytes 12292
  58.3 113.9 %copy-start.72 = (f32[768]{0:T(1024)}, f32[768]{0:T(1024)S(1)}, u32[]{:S(2)}) copy-start(f32[768]{0:T(1024)S(1)} %get-tuple-element.308) | copy-start | bytes 9220
  66.9 44.3 %copy-start.92 = (f32[3,64]{1,0:T(4,128)}, f32[3,64]{1,0:T(4,128)S(1)}, u32[]{:S(2)}) copy-start(f32[3,64]{1,0:T(4,128)S(1)} %add.397) | copy-start | bytes 2308
  102.8 15.4 %copy-start.14 = (pred[1024,1024]{0,1:T(8,128)(4,1)}, pred[1024,1024]{0,1:T(8,128)(4,1)S(1)}, u32[]{:S(2)}) copy-start(pred[1024,1024]{0,1:T(8,128)(4,1)S(1)} %fusion.21) | copy-start | bytes 3145732
  127.4 113.1 %all-reduce.19.cloned.1.call-start = ((), (), s32[]{:S(2)}) async-start(), calls=%async_computation.9 | async-start | bytes 3145728 | tf_op jit(solution)/shard_map/psum | solution.py:166
  128.3 45.3 %copy-start.78 = (f32[1024]{0:T(1024)}, f32[1024]{0:T(1024)S(1)}, u32[]{:S(2)}) copy-start(f32[1024]{0:T(1024)S(1)} %broadcast_multiply_fusion.1) | copy-start | bytes 12292
  173.9 14.4 %copy-start.39 = (f32[1024,1,192]{0,2,1:T(8,128)}, f32[1024,1,192]{0,2,1:T(8,128)S(1)}, u32[]{:S(2)}) copy-start(f32[1024,1,192]{0,2,1:T(8,128)S(1)} %get-tuple-element.273) | copy-start | bytes 2359300
  197.3 48.6 %all-gather.3.cloned.1.call-start = ((), (), s32[]{:S(2)}) async-start(), calls=%async_computation.7 | async-start | bytes 1327104 | tf_op jit(solution)/shard_map/all_gather | solution.py:161
  197.9 85.6 %all-gather.5.cloned.1.call-start = ((), (), s32[]{:S(2)}) async-start(), calls=%async_computation.8 | async-start | bytes 1327104 | tf_op jit(solution)/shard_map/all_gather | solution.py:162
  198.5 168.4 %all-reduce.31.cloned.1.call-start = ((), (), s32[]{:S(2)}) async-start(), calls=%async_computation.15 | async-start | bytes 6291456 | tf_op jit(solution)/shard_map/psum | solution.py:166
  305.8 137.1 %all-to-all-start.3 = ((bf16[8,768,96]{1,2,0:T(8,128)(2,1)}), bf16[8,768,96]{1,2,0:T(8,128)(2,1)}, u32[]{:S(2)}, u32[]{:S(2)}) async-start(bf16[8,768,96]{1,2,0:T(8,128)(2,1)} %bitcast.222), calls=%async_computation.3 | async-start | bytes 2359296 | tf_op jit(solution)/shard_map/all_to_all | solution.py:34
  390.8 13.3 %slice-start = ((s8[12582912]{0:T(1024)(128)(4,1)}), s8[4194304]{0:T(1024)(128)(4,1)S(1)}, s32[]{:S(2)}) async-start(s8[12582912]{0:T(1024)(128)(4,1)} %bitcast.187), calls=%async_computation.16 | async-start | bytes 8388608
  390.8 13.3 %slice-start.1 = ((s8[12582912]{0:T(1024)(128)(4,1)}), s8[4194304]{0:T(1024)(128)(4,1)S(1)}, s32[]{:S(2)}) async-start(s8[12582912]{0:T(1024)(128)(4,1)} %bitcast.187), calls=%async_computation.17 | async-start | bytes 8388608
  390.8 13.3 %slice-start.2 = ((s8[12582912]{0:T(1024)(128)(4,1)}), s8[4194304]{0:T(1024)(128)(4,1)S(1)}, s32[]{:S(2)}) async-start(s8[12582912]{0:T(1024)(128)(4,1)} %bitcast.187), calls=%async_computation.18 | async-start | bytes 8388608
  390.8 13.3 %copy-start.68 = (f32[3,1024]{1,0:T(4,128)S(1)}, f32[3,1024]{1,0:T(4,128)}, u32[]{:S(2)}) copy-start(f32[3,1024]{1,0:T(4,128)} %log_add_fusion.1) | copy-start | bytes 36868
  414.1 16.0 %slice-start.6 = ((s8[12582912]{0:T(1024)(128)(4,1)}), s8[4194304]{0:T(1024)(128)(4,1)S(1)}, s32[]{:S(2)}) async-start(s8[12582912]{0:T(1024)(128)(4,1)} %bitcast.191), calls=%async_computation.22 | async-start | bytes 8388608
  414.1 13.4 %copy-start.35 = (bf16[1024,1,192]{0,2,1:T(8,128)(2,1)S(1)}, bf16[1024,1,192]{0,2,1:T(8,128)(2,1)}, u32[]{:S(2)}) copy-start(bf16[1024,1,192]{0,2,1:T(8,128)(2,1)} %slice.392) | copy-start | bytes 1179652
  414.1 15.9 %slice-start.7 = ((s8[12582912]{0:T(1024)(128)(4,1)}), s8[4194304]{0:T(1024)(128)(4,1)S(1)}, s32[]{:S(2)}) async-start(s8[12582912]{0:T(1024)(128)(4,1)} %bitcast.191), calls=%async_computation.23 | async-start | bytes 8388608
  414.1 15.9 %slice-start.8 = ((s8[12582912]{0:T(1024)(128)(4,1)}), s8[4194304]{0:T(1024)(128)(4,1)S(1)}, s32[]{:S(2)}) async-start(s8[12582912]{0:T(1024)(128)(4,1)} %bitcast.191), calls=%async_computation.24 | async-start | bytes 8388608
  442.8 34.1 %all-to-all-start.2 = ((bf16[8,96,768]{2,1,0:T(8,128)(2,1)}), bf16[8,96,768]{2,1,0:T(8,128)(2,1)}, u32[]{:S(2)}, u32[]{:S(2)}) async-start(bf16[8,96,768]{2,1,0:T(8,128)(2,1)} %bitcast.220), calls=%async_computation.2 | async-start | bytes 2359296 | tf_op jit(solution)/shard_map/all_to_all | solution.py:34
  448.4 13.0 %slice-start.3 = ((s8[12582912]{0:T(1024)(128)(4,1)}), s8[4194304]{0:T(1024)(128)(4,1)S(1)}, s32[]{:S(2)}) async-start(s8[12582912]{0:T(1024)(128)(4,1)} %bitcast.189), calls=%async_computation.19 | async-start | bytes 8388608
  476.9 15.5 %all-to-all-start.1 = ((bf16[8,192,96]{2,1,0:T(8,128)(2,1)}), bf16[8,192,96]{2,1,0:T(8,128)(2,1)S(1)}, u32[]{:S(2)}, u32[]{:S(2)}) async-start(bf16[8,192,96]{2,1,0:T(8,128)(2,1)} %bitcast.186), calls=%async_computation.1 | async-start | bytes 786432 | tf_op jit(solution)/shard_map/all_to_all | solution.py:34
  492.4 33.5 %all-to-all-start = ((bf16[8,3,96,192]{2,3,1,0:T(8,128)(2,1)}), bf16[8,3,96,192]{2,3,1,0:T(8,128)(2,1)}, u32[]{:S(2)}, u32[]{:S(2)}) async-start(bf16[8,3,96,192]{2,3,1,0:T(8,128)(2,1)} %bitcast.198), calls=%async_computation | async-start | bytes 2359296 | tf_op jit(solution)/shard_map/all_to_all | solution.py:34
  497.5 106.5 %all-reduce.21.cloned.1.call-start = ((), (), s32[]{:S(2)}) async-start(), calls=%async_computation.10 | async-start | bytes 2359296 | tf_op jit(solution)/shard_map/psum | solution.py:120
  568.5 98.4 %all-reduce.23.cloned.1.call-start = ((), (), s32[]{:S(2)}) async-start(), calls=%async_computation.11 | async-start | bytes 2359296 | tf_op jit(solution)/shard_map/psum | solution.py:120
  629.2 93.2 %all-reduce.25.cloned.1.call-start = ((), (), s32[]{:S(2)}) async-start(), calls=%async_computation.12 | async-start | bytes 2359296 | tf_op jit(solution)/shard_map/psum | solution.py:120
  684.7 93.0 %all-reduce.27.cloned.1.call-start = ((), (), s32[]{:S(2)}) async-start(), calls=%async_computation.13 | async-start | bytes 2359296 | tf_op jit(solution)/shard_map/psum | solution.py:120
  740.0 195.2 %all-reduce.29.cloned.1.call-start = ((), (), s32[]{:S(2)}) async-start(), calls=%async_computation.14 | async-start | bytes 14942208 | tf_op jit(solution)/shard_map/psum | solution.py:166
  795.4 139.8 %copy-start.74 = (f32[768]{0:T(1024)S(1)}, f32[768]{0:T(1024)}, u32[]{:S(2)}) copy-start(f32[768]{0:T(1024)} %copy-done.72) | copy-start | bytes 9220
  795.4 139.8 %copy-start.77 = (f32[1024]{0:T(1024)S(1)}, f32[1024]{0:T(1024)}, u32[]{:S(2)}) copy-start(f32[1024]{0:T(1024)} %copy-done.75) | copy-start | bytes 12292
  795.4 139.8 %copy-start.79 = (f32[1024]{0:T(1024)S(1)}, f32[1024]{0:T(1024)}, u32[]{:S(2)}) copy-start(f32[1024]{0:T(1024)} %copy-done.78) | copy-start | bytes 12292
  940.6 13.0 %copy-start.101 = (f32[1024]{0:T(1024)S(1)}, f32[1024]{0:T(1024)}, u32[]{:S(2)}) copy-start(f32[1024]{0:T(1024)} %copy-done.99) | copy-start | bytes 12292
  940.6 13.0 %copy-start.103 = (f32[1024]{0:T(1024)S(1)}, f32[1024]{0:T(1024)}, u32[]{:S(2)}) copy-start(f32[1024]{0:T(1024)} %copy-done.102) | copy-start | bytes 12292
  940.6 13.0 %copy-start.136 = (f32[768]{0:T(1024)S(1)}, f32[768]{0:T(1024)}, u32[]{:S(2)}) copy-start(f32[768]{0:T(1024)} %get-tuple-element.226) | copy-start | bytes 9220
  947.8 77.1 %all-to-all-start.5 = ((bf16[8,96,768]{2,1,0:T(8,128)(2,1)}), bf16[8,96,768]{2,1,0:T(8,128)(2,1)}, u32[]{:S(2)}, u32[]{:S(2)}) async-start(bf16[8,96,768]{2,1,0:T(8,128)(2,1)} %bitcast.221), calls=%async_computation.5 | async-start | bytes 2359296 | tf_op jit(solution)/shard_map/all_to_all | solution.py:333
  953.7 51.4 %copy-start.145 = (f32[2,192]{1,0:T(2,128)S(1)}, f32[2,192]{1,0:T(2,128)}, u32[]{:S(2)}) copy-start(f32[2,192]{1,0:T(2,128)} %param.42) | copy-start | bytes 4612
  953.7 51.4 %copy-start.161 = (f32[2,192]{1,0:T(2,128)S(1)}, f32[2,192]{1,0:T(2,128)}, u32[]{:S(2)}) copy-start(f32[2,192]{1,0:T(2,128)} %param.50) | copy-start | bytes 4612
  953.7 52.0 %copy-start.152 = (f32[768]{0:T(1024)S(1)}, f32[768]{0:T(1024)}, u32[]{:S(2)}) copy-start(f32[768]{0:T(1024)} %param.43) | copy-start | bytes 9220
  953.7 52.0 %copy-start.153 = (f32[768]{0:T(1024)S(1)}, f32[768]{0:T(1024)}, u32[]{:S(2)}) copy-start(f32[768]{0:T(1024)} %param.51) | copy-start | bytes 9220
  953.8 52.6 %copy-start.83 = (f32[1024]{0:T(1024)S(1)}, f32[1024]{0:T(1024)}, u32[]{:S(2)}) copy-start(f32[1024]{0:T(1024)} %copy-done.82) | copy-start | bytes 12292
  953.8 52.5 %copy-start.89 = (f32[1024]{0:T(1024)S(1)}, f32[1024]{0:T(1024)}, u32[]{:S(2)}) copy-start(f32[1024]{0:T(1024)} %fusion.148) | copy-start | bytes 12292
  953.8 52.5 %copy-start.107 = (f32[1024]{0:T(1024)S(1)}, f32[1024]{0:T(1024)}, u32[]{:S(2)}) copy-start(f32[1024]{0:T(1024)} %copy-done.106) | copy-start | bytes 12292
  953.8 52.5 %copy-start.126 = (bf16[1024]{0:T(1024)(128)(2,1)S(1)}, bf16[1024]{0:T(1024)(128)(2,1)}, u32[]{:S(2)}) copy-start(bf16[1024]{0:T(1024)(128)(2,1)} %get-tuple-element.307) | copy-start | bytes 6148
  (155 other events, 713.0 us)
Sparse Core Ops, SparseCore 0:
  127.5 41.5 all-reduce.16
  197.5 42.9 all-reduce.18
  299.7 67.1 all-reduce.30
  568.6 35.3 all-reduce.20
  629.3 37.5 all-reduce.22
  684.8 37.5 all-reduce.24
  740.1 37.5 all-reduce.26
  795.6 139.6 all-reduce.28
Sparse Core Ops, SparseCore 1:
  200.0 41.4 all-gather.2
  243.5 40.0 all-gather.4
where the time goes:
time: 1050 us; the launch traced here: 1040 us
  waiting for transfers between devices  449 us (43%)
  matrix products  230 us (22%)
  blocking collectives  146 us (14%)
  other arithmetic  124 us (12%)
  local copies, waits for them, and re-layouts  43.6 us (4%)
  starting transfers between devices  25.6 us (2%)
  between operations  19.1 us (2%)
    psum x4, waiting for transfers between devices, across_heads(): lax.psum(partial_value.astype(jnp.bfloat16), 'mp').astype(jnp.float32)  259 us
    psum x4, waiting for transfers between devices, newton(): lax.psum(highest(current, current.T).astype(jnp.bfloat16), 'mp')  132 us
    dot_general x15, matrix products, highest(): jnp.dot(left, right, precision=lax.Precision.HIGHEST, preferred_element_t...  78.4 us
    psum x1, blocking collectives, on_device(): gains_sum, biases_sum, heads_sum, units_sum = lax.psum(vectors, 'dp')  42.3 us
    all_gather x1, blocking collectives, fetch(): lax.all_gather(qkv_weight, 'dp', axis=1, tiled=True)  40.3 us
    all_to_all x1, blocking collectives, on_device(): lax.all_to_all(outgoing.astype(jnp.bfloat16), 'dp', split_axis=0, concat_...  32.4 us
    all_to_all x4, waiting for transfers between devices, summed_on_arrival(): lax.all_to_all(blocks, axis, split_axis=0, concat_axis=0, tiled=True)  31.6 us
    all_gather x1, blocking collectives, fetch(): lax.all_gather(out_weight, 'dp', axis=1, tiled=True)  31.4 us
  transfers between devices with their start and end apart: 15, of which 12 were waited for; matrix products, arithmetic and copies ran while one was open for 19% of the time, Pallas kernels for 0%

commit v1 on v0

v1 whole, which is shorter than its diff:
```python
import math

import jax
import jax.numpy as jnp
from jax import lax
from jax.sharding import Mesh, PartitionSpec as P

D = 768
HEAD_DIM = 64
FF = 3072
SLOTS = 1024
NS_STEPS = 5

EPS = 1e-05
MOMENTUM = 0.9
NS_A = 3.4445
NS_B = -4.775
NS_C = 2.0315
RATE = 1.0
DECAY = 0.01
VECTOR_RATE = 0.1
FLOOR = -1e30

BF = jnp.bfloat16
F32 = jnp.float32


def swap(value, axis, distance=1):
    size = lax.axis_size(axis)
    return lax.ppermute(value, axis, [(i, i ^ distance) for i in range(size)])


def join(mine, theirs, bit, dim):
    low = jnp.where(bit, theirs, mine)
    high = jnp.where(bit, mine, theirs)
    return jnp.stack((low, high), axis=dim)


def distances(axis):
    found = []
    step = lax.axis_size(axis) // 2
    while step >= 1:
        found.append(step)
        step //= 2
    return found


def bit_of(axis, distance=1):
    return (lax.axis_index(axis) // distance) % 2 == 1


def gather_z(piece):
    lead = 0
    for distance in distances("z"):
        piece = join(piece, swap(piece, "z", distance), bit_of("z", distance), lead)
        lead += 1
    return piece.reshape(lax.axis_size("z"), *piece.shape[lead:])


def gather_rows(shard):
    half = shard.shape[0] // 2
    first = gather_z(shard[:half])
    second = gather_z(shard[half:])
    first = join(first, swap(first, "y"), bit_of("y"), 1)
    first = jnp.stack((first, swap(first, "x")))
    second = jnp.stack((second, swap(second, "x")))
    second = join(second, swap(second, "y"), bit_of("y"), 2)
    return jnp.stack((first, second), axis=3).reshape(2, -1, shard.shape[1])


def take(value, bit, dim):
    low, high = (lax.index_in_dim(value, k, dim, keepdims=False) for k in (0, 1))
    keep = jnp.where(bit, high, low)
    send = jnp.where(bit, low, high)
    return keep, send


def halve(value, axis, bit, dim, distance=1):
    keep, send = take(value, bit, dim)
    return keep.astype(F32) + swap(send.astype(BF), axis, distance).astype(F32)


def scatter_z(value):
    steps = distances("z")
    value = value.reshape(*(2 for _ in steps), *value.shape[1:])
    for k in range(len(steps) - 1, -1, -1):
        value = halve(value, "z", bit_of("z", steps[k]), k, steps[k])
    return value


def scatter_rows(grad):
    width = grad.shape[2]
    planes = lax.axis_size("z")
    parts = grad.reshape(2, planes, 2, 2, -1, width)
    first, second = parts[:, :, :, 0], parts[:, :, :, 1]
    first = first[0].astype(F32) + swap(first[1], "x").astype(F32)
    first = halve(first, "y", bit_of("y"), 1)
    second = halve(second, "y", bit_of("y"), 2)
    second = second[0] + swap(second[1].astype(BF), "x").astype(F32)
    return jnp.concatenate((scatter_z(first), scatter_z(second)), axis=0)


def fixed(value):
    return lax.optimization_barrier(value.astype(BF))


def across_cores(partial_value):
    own = fixed(partial_value)
    return own.astype(F32) + swap(own, "c").astype(F32)


def both_bins(value):
    own = fixed(value)
    half = SLOTS // 2
    core = lax.axis_index("c")
    sent = lax.dynamic_slice_in_dim(own, core * half, half, axis=0)
    got = swap(sent, "x")
    other = join(got, swap(got, "c"), bit_of("c"), 0).reshape(value.shape)
    return join(own, other, bit_of("x"), 0).reshape(-1, D).astype(F32)


def highest(left, right):
    return jnp.dot(left, right, precision=lax.Precision.HIGHEST, preferred_element_type=F32)


def layer_norm(rows, gain, shift):
    centre = rows - jnp.mean(rows, axis=-1, keepdims=True)
    spread = jnp.mean(centre * centre, axis=-1, keepdims=True)
    return centre * lax.rsqrt(spread + EPS) * gain + shift


def segments_of(seq_lengths, seq_bin, index):
    count = seq_lengths.shape[0]
    order = jnp.arange(count, dtype=jnp.int32)
    inside = seq_bin == index
    leader = jnp.min(jnp.where(inside, order, count))
    first = jnp.sum(jnp.where(order == leader, seq_lengths, 0))
    total = jnp.sum(jnp.where(inside, seq_lengths, 0))
    slot = jnp.arange(SLOTS, dtype=jnp.int32)
    segment = jnp.where(slot < first, 0, jnp.where(slot < total, 1, slot + 2))
    return (segment, slot < total)


def causal_mask(segment):
    order = jnp.arange(segment.shape[0], dtype=jnp.int32)
    return (segment[:, None] == segment[None, :]) & (order[None, :] <= order[:, None])


def split_heads(block):
    return block.reshape(block.shape[0], block.shape[1] // HEAD_DIM, HEAD_DIM)


def attend(query, keys, values, causal):
    scores = jnp.einsum(
        "qhd,khd->hqk", split_heads(query), split_heads(keys), preferred_element_type=F32
    )
    scores = jnp.where(causal[None], scores, FLOOR)
    top = jnp.max(scores, axis=-1, keepdims=True)
    raised = jnp.exp(scores - top)
    total = jnp.sum(raised, axis=-1, keepdims=True)
    weights = (raised / total).astype(BF)
    mixed = jnp.einsum("hqk,khd->qhd", weights, split_heads(values), preferred_element_type=F32)
    return (mixed.reshape(query.shape), top + jnp.log(total))


def attend_back(query, keys, values, log_total, causal, grad_mixed):
    heads_query = split_heads(query)
    heads_keys = split_heads(keys)
    heads_values = split_heads(values)
    grad_heads = split_heads(grad_mixed)
    scores = jnp.einsum("qhd,khd->hqk", heads_query, heads_keys, preferred_element_type=F32)
    weights = jnp.where(causal[None], jnp.exp(scores - log_total), 0.0)
    grad_values = jnp.einsum(
        "hqk,qhd->khd", weights.astype(BF), grad_heads, preferred_element_type=F32
    )
    grad_weights = jnp.einsum("qhd,khd->hqk", grad_heads, heads_values, preferred_element_type=F32)
    inner = jnp.sum(weights * grad_weights, axis=-1, keepdims=True)
    grad_scores = (weights * (grad_weights - inner)).astype(BF)
    grad_query = jnp.einsum("hqk,khd->qhd", grad_scores, heads_keys, preferred_element_type=F32)
    grad_keys = jnp.einsum("hqk,qhd->khd", grad_scores, heads_query, preferred_element_type=F32)
    shape = query.shape
    return (
        grad_query.reshape(shape).astype(BF),
        grad_keys.reshape(shape).astype(BF),
        grad_values.reshape(shape).astype(BF),
    )


def gram_sum(gram):
    parts = gram.reshape(2, D // 2, D)
    keep, send = take(parts, bit_of("c"), 0)
    mine = keep + swap(send, "c")
    mine = mine + swap(mine, "x")
    return join(mine, swap(mine, "c"), bit_of("c"), 0).reshape(D, D)


def newton(panel):
    gram = gram_sum(highest(panel, panel.T))
    factor = 1.0 / (jnp.sqrt(jnp.trace(gram)) + 1e-07)
    gram = gram * (factor * factor)
    eye = jnp.eye(D, dtype=F32)
    total = None
    for step in range(NS_STEPS):
        poly = NS_A * eye + NS_B * gram + NS_C * highest(gram, gram)
        total = poly if total is None else highest(poly, total)
        if step < NS_STEPS - 1:
            gram = highest(highest(poly, gram), poly)
    return highest(total, panel * factor)


def on_device(
    tokens,
    cotangent,
    seq_lengths,
    seq_bin,
    qkv_weight,
    out_weight,
    up_weight,
    down_weight,
    norm_gains,
    shared_biases,
    head_biases,
    unit_bias,
    qkv_moment,
    out_moment,
    up_moment,
    down_moment,
    gain_moment,
    bias_moment,
    head_moment,
    unit_moment,
):
    x_index = lax.axis_index("x")
    groups = lax.axis_size("z") * lax.axis_size("y")
    position = lax.axis_index("z") * lax.axis_size("y") + lax.axis_index("y")
    rows_each = qkv_weight.shape[1]
    heads_each = qkv_weight.shape[2]
    units_each = up_weight.shape[1]
    scale = HEAD_DIM ** (-0.5)

    qkv_shard = jnp.moveaxis(qkv_weight, 0, 1).reshape(rows_each, 3 * heads_each)
    qkv_full = gather_rows(qkv_shard)
    rest = gather_rows(jnp.concatenate((out_weight.T, up_weight), axis=1))
    down_full = gather_rows(down_weight.T)
    out_full = rest[:, :, :heads_each]
    up_full = rest[:, :, heads_each:]

    small = jnp.concatenate((head_biases.reshape(-1), unit_bias))
    small = jnp.stack((small, swap(small, "x")))
    query_bias = small[:, :heads_each].reshape(-1)
    value_bias = small[:, heads_each : 2 * heads_each].reshape(-1)
    units_shift = small[:, 2 * heads_each :].reshape(-1)

    start = x_index * SLOTS
    rows = lax.dynamic_slice_in_dim(tokens, start, SLOTS, axis=0)
    segment, valid = segments_of(seq_lengths, seq_bin, position * 2 + x_index)
    causal = causal_mask(segment)
    source = rows.astype(F32)
    normed = layer_norm(source, norm_gains[0], shared_biases[0]).astype(BF)
    weights_qkv = qkv_full.reshape(2, D, 3, heads_each)
    project = jnp.einsum("rd,gdtc->rtgc", normed, weights_qkv, preferred_element_type=F32)
    project = project.reshape(SLOTS, 3, 2 * heads_each)
    query = ((project[:, 0] + query_bias) * scale).astype(BF)
    keys = project[:, 1].astype(BF)
    values = (project[:, 2] + value_bias).astype(BF)
    mixed, log_total = attend(query, keys, values, causal)
    mixed = mixed.astype(BF)
    mixed_two = mixed.reshape(SLOTS, 2, heads_each)
    branch = across_cores(
        jnp.einsum("rgc,gdc->rd", mixed_two, out_full, preferred_element_type=F32)
    )
    hidden = source + (branch + shared_biases[2])
    normed_two = layer_norm(hidden, norm_gains[1], shared_biases[1]).astype(BF)
    up_cols = jnp.concatenate((up_full[0], up_full[1]), axis=1)
    down_cols = jnp.concatenate((down_full[0], down_full[1]), axis=1)
    before = jnp.dot(normed_two, up_cols, preferred_element_type=F32) + units_shift
    active = jax.nn.gelu(before).astype(BF)
    result = hidden + (
        across_cores(jnp.einsum("ru,du->rd", active, down_cols, preferred_element_type=F32))
        + shared_biases[3]
    )
    block_out = both_bins(result)

    grad_rows = lax.dynamic_slice_in_dim(cotangent, start, SLOTS, axis=0)
    grad_rows = grad_rows * valid[:, None].astype(BF)
    grad_result = grad_rows.astype(F32)
    grad_down = jnp.einsum("rd,ru->du", grad_rows, active, preferred_element_type=F32).astype(BF)
    grad_down = jnp.stack((grad_down[:, :units_each], grad_down[:, units_each:]))
    sum_down = scatter_rows(grad_down)
    grad_active = jnp.dot(grad_rows, down_cols, preferred_element_type=F32)
    grad_before = jax.vjp(jax.nn.gelu, before)[1](grad_active)[0].astype(BF)
    grad_up = jnp.einsum("rd,ru->du", normed_two, grad_before, preferred_element_type=F32).astype(BF)
    grad_up = jnp.stack((grad_up[:, :units_each], grad_up[:, units_each:]))
    sum_up = scatter_rows(grad_up)
    grad_normed_two = across_cores(
        jnp.einsum("ru,du->rd", grad_before, up_cols, preferred_element_type=F32)
    )
    grad_hidden, grad_gain_two, grad_shift_two = jax.vjp(
        layer_norm, hidden, norm_gains[1], shared_biases[1]
    )[1](grad_normed_two)
    grad_hidden = grad_hidden + grad_result
    grad_branch = grad_hidden.astype(BF)
    grad_out = jnp.einsum("rd,rgc->gdc", grad_branch, mixed_two, preferred_element_type=F32)
    grad_mixed = jnp.einsum("rd,gdc->rgc", grad_branch, out_full, preferred_element_type=F32)
    grad_mixed = grad_mixed.astype(BF).reshape(SLOTS, 2 * heads_each)
    grad_query, grad_keys, grad_values = attend_back(
        query, keys, values, log_total, causal, grad_mixed
    )
    grad_query = (grad_query.astype(F32) * scale).astype(BF)
    stacked = jnp.stack((grad_query, grad_keys, grad_values), axis=1)
    stacked = stacked.reshape(SLOTS, 3, 2, heads_each)
    grad_qkv = jnp.einsum("rd,rtgc->gdtc", normed, stacked, preferred_element_type=F32)
    grad_square = jnp.concatenate(
        (grad_qkv.astype(BF).reshape(2, D, 3 * heads_each), grad_out.astype(BF)), axis=2
    )
    sum_square = scatter_rows(grad_square)
    grad_normed = across_cores(
        jnp.einsum("rtgc,gdtc->rd", stacked, weights_qkv, preferred_element_type=F32)
    )
    grad_source, grad_gain_one, grad_shift_one = jax.vjp(
        layer_norm, source, norm_gains[0], shared_biases[0]
    )[1](grad_normed)
    input_grad = both_bins(grad_hidden + grad_source)

    def by_x(value):
        mine, theirs = value[:, 0], value[:, 1]
        return join(mine, theirs, bit_of("x"), 1)

    grad_heads = jnp.stack(
        (jnp.sum(grad_query.astype(F32), axis=0), jnp.sum(grad_values.astype(F32), axis=0))
    )
    grad_units = jnp.sum(grad_before.astype(F32), axis=0)
    vectors = (
        jnp.stack((grad_gain_one, grad_gain_two)),
        jnp.stack(
            (
                grad_shift_one,
                grad_shift_two,
                jnp.sum(grad_branch.astype(F32), axis=0),
                jnp.sum(grad_result, axis=0),
            )
        ),
        by_x(grad_heads.reshape(2, 2, heads_each)),
        by_x(grad_units.reshape(1, 2, units_each)),
    )
    sizes = [v.size for v in vectors]
    flat = lax.psum(jnp.concatenate([v.reshape(-1) for v in vectors]), ("z", "y", "x"))
    ends = [sum(sizes[: k + 1]) for k in range(4)]
    pieces = [flat[end - size : end] for end, size in zip(ends, sizes)]
    gains_sum = pieces[0].reshape(2, D)
    biases_sum = pieces[1].reshape(4, D)
    heads_sum = lax.dynamic_index_in_dim(
        pieces[2].reshape(2, 2, heads_each), x_index, 1, keepdims=False
    )
    units_sum = lax.dynamic_index_in_dim(pieces[3].reshape(2, units_each), x_index, 0, False)

    grads = (
        sum_square[:, :heads_each],
        sum_square[:, heads_each : 2 * heads_each],
        sum_square[:, 2 * heads_each : 3 * heads_each],
        sum_square[:, 3 * heads_each :],
        sum_up,
        sum_down,
    )
    moments = (
        qkv_moment[0],
        qkv_moment[1],
        qkv_moment[2],
        out_moment.T,
        up_moment,
        down_moment.T,
    )
    next_moments = [MOMENTUM * moment + grad for moment, grad in zip(moments, grads)]
    local_panels = [grad + MOMENTUM * moment for moment, grad in zip(next_moments, grads)]
    spacing = groups // 6
    width_all = units_each
    outgoing = jnp.zeros((groups, rows_each, width_all), BF)
    for number in range(6):
        shard = local_panels[number].astype(BF)
        shard = jnp.pad(shard, ((0, 0), (0, width_all - shard.shape[1])))
        outgoing = outgoing.at[number * spacing].set(shard)
    incoming = lax.all_to_all(outgoing, ("z", "y"), split_axis=0, concat_axis=0, tiled=True)
    orth = newton(incoming.reshape(groups * rows_each, width_all).astype(F32))
    back = lax.all_to_all(
        orth.astype(BF).reshape(groups, rows_each, width_all),
        ("z", "y"),
        split_axis=0,
        concat_axis=0,
        tiled=True,
    ).astype(F32)
    returned = [back[number * spacing][:, : local_panels[number].shape[1]] for number in range(6)]
    keep_share = 1.0 - RATE * DECAY
    up_factor = math.sqrt(max(1.0, FF / D))
    qkv_next = qkv_weight.astype(F32) * keep_share - RATE * jnp.stack(returned[:3])
    out_next = out_weight.astype(F32) * keep_share - RATE * returned[3].T
    up_next = up_weight.astype(F32) * keep_share - RATE * up_factor * returned[4]
    down_next = down_weight.astype(F32) * keep_share - RATE * returned[5].T
    rate_vector = VECTOR_RATE / math.sqrt(groups * tokens.shape[0])
    gain_moment_next = MOMENTUM * gain_moment + gains_sum
    bias_moment_next = MOMENTUM * bias_moment + biases_sum
    head_moment_next = MOMENTUM * head_moment + heads_sum
    unit_moment_next = MOMENTUM * unit_moment + units_sum
    gain_next = norm_gains - rate_vector * gain_moment_next
    bias_next = shared_biases - rate_vector * bias_moment_next
    head_next = head_biases - rate_vector * head_moment_next
    unit_next = unit_bias - rate_vector * unit_moment_next
    return (
        block_out,
        input_grad,
        jnp.stack(next_moments[:3]),
        qkv_next,
        next_moments[3].T,
        out_next,
        next_moments[4],
        up_next,
        next_moments[5].T,
        down_next,
        gain_moment_next,
        gain_next,
        bias_moment_next,
        bias_next,
        head_moment_next,
        head_next,
        unit_moment_next,
        unit_next,
    )


def solution(mesh):
    dp_size, mp_size = mesh.devices.shape
    split = Mesh(
        mesh.devices.reshape(dp_size // 2, 2, mp_size // 2, 2), ("z", "y", "x", "c")
    )
    dp, mp = ("z", "y"), ("x", "c")
    in_specs = (
        P(dp, None),
        P(dp, None),
        P(),
        P(),
        P(None, dp, mp),
        P(mp, dp),
        P(dp, mp),
        P(mp, dp),
        P(),
        P(),
        P(None, mp),
        P(mp),
        P(None, dp, mp),
        P(mp, dp),
        P(dp, mp),
        P(mp, dp),
        P(),
        P(),
        P(None, mp),
        P(mp),
    )
    out_specs = (
        P(dp, None),
        P(dp, None),
        P(None, dp, mp),
        P(None, dp, mp),
        P(mp, dp),
        P(mp, dp),
        P(dp, mp),
        P(dp, mp),
        P(mp, dp),
        P(mp, dp),
        P(),
        P(),
        P(),
        P(),
        P(None, mp),
        P(None, mp),
        P(mp),
        P(mp),
    )
    return jax.shard_map(
        on_device, mesh=split, in_specs=in_specs, out_specs=out_specs, check_vma=False
    )
```

time: 1050 us -> 733 us (0.70)
  waiting for transfers between devices: 449 us -> 165 us
  blocking collectives: 146 us -> 74.3 us
  starting transfers between devices: 25.6 us -> 72.9 us
  local copies, waits for them, and re-layouts: 43.6 us -> 69.6 us
  between operations: 19.1 us -> 3.67 us
  other arithmetic: 124 us -> 112 us
    psum x8 -> x0, waiting for transfers between devices: 392 us -> none  [the longest x4 259 us: across_heads(): lax.psum(partial_value.astype(jnp.bfloat16), 'mp').astype(jnp.float32)]
    ppermute x0 -> x60, waiting for transfers between devices: none -> 132 us  [swap(): return lax.ppermute(value, axis, [(i, i ^ distance) for i in range(size)])]
    all_gather x2 -> x0, blocking collectives: 71.7 us -> none  [the longest x1 40.3 us: fetch(): lax.all_gather(qkv_weight, 'dp', axis=1, tiled=True)]
    ppermute x0 -> x60, starting transfers between devices: none -> 62.7 us  [swap(): return lax.ppermute(value, axis, [(i, i ^ distance) for i in range(size)])]
    dot_general x15 -> x19, matrix products: 78.4 us -> 117 us  [highest(): jnp.dot(left, right, precision=lax.Precision.HIGHEST, preferred_element_t...]
    all_to_all x1 -> x0, blocking collectives: 32.4 us -> none  [on_device(): lax.all_to_all(outgoing.astype(jnp.bfloat16), 'dp', split_axis=0, concat_...]
    psum x1, blocking collectives: 42.3 us -> 74.3 us  [on_device(): lax.psum(jnp.concatenate([v.reshape(-1) for v in vectors]), ('z', 'y', 'x'))]
    all_gather x2 -> x0, waiting for transfers between devices: 25 us -> none  [the longest x1 25 us: fetch(): lax.all_gather(down_weight, 'dp', axis=1, tiled=True)]
  transfers between devices with their start and end apart: 15 -> 62, of which waited for: 12 -> 30; matrix products, arithmetic and copies ran while one was open for 19% -> 38% of each run, Pallas kernels for 0% -> 0%
where the time goes in v1:
time: 733 us; the launch traced here: 726 us
  matrix products  229 us (31%)
  waiting for transfers between devices  165 us (23%)
  other arithmetic  112 us (15%)
  blocking collectives  74.3 us (10%)
  starting transfers between devices  72.9 us (10%)
  local copies, waits for them, and re-layouts  69.6 us (9%)
    ppermute x60, waiting for transfers between devices, swap(): return lax.ppermute(value, axis, [(i, i ^ distance) for i in range(size)])  132 us
    dot_general x19, matrix products, highest(): jnp.dot(left, right, precision=lax.Precision.HIGHEST, preferred_element_t...  117 us
    psum x1, blocking collectives, on_device(): lax.psum(jnp.concatenate([v.reshape(-1) for v in vectors]), ('z', 'y', 'x'))  74.3 us
    ppermute x60, starting transfers between devices, swap(): return lax.ppermute(value, axis, [(i, i ^ distance) for i in range(size)])  62.7 us
    all_to_all x1, waiting for transfers between devices, on_device(): lax.all_to_all(orth.astype(BF).reshape(groups, rows_each, width_all), ('z...  21.6 us
    dot_general x1, matrix products, attend_back(): jnp.einsum('qhd,khd->hqk', grad_heads, heads_values, preferred_element_ty...  21.3 us
    convert_element_type x1, other arithmetic, attend_back(): grad_scores = (weights * (grad_weights - inner)).astype(BF)  18.2 us
    unnamed x182, local copies, waits for them, and re-layouts  15.4 us
  transfers between devices with their start and end apart: 62, of which 30 were waited for; matrix products, arithmetic and copies ran while one was open for 38% of the time, Pallas kernels for 0%

profile of v1, /device:TPU:0, one launch (start us, length us, event | category | flops | bytes accessed | tf_op | source)
XLA Modules:
  0.0 725.8 jit_solution(11167456791730699767)
XLA Ops:
  51.6 5.6 collective-permute-done.14
  69.9 5.7 collective-permute-done.11
  80.0 7.9 %collective-permute-done.3 = bf16[4,2,48,576]{3,2,0,1:T(8,128)(2,1)S(1)} collective-permute-done((bf16[4,2,48,576]{3,2,0,1:T(8,128)(2,1)S(1)}, bf16[4,2,48,576]{3,2,0,1:T(8,128)(2,1)S(1)}, u32[]{:S(2)}, u32[]{:S(2)}) %collective-permute-start.3) | collective-permute-done | bytes 442400 | tf_op jit(solution)/shard_map/ppermute | solution.py:30
  89.0 7.8 %copy.218 = bf16[2,4,2,2,48,576]{4,3,2,1,5,0:T(2,128)(2,1)} copy(bf16[2,4,2,2,48,576]{5,4,2,1,0,3:T(8,128)(2,1)S(1)} %pad_maximum_fusion.7) | data formatting | bytes 3538944 | tf_op jit(solution)/shard_map/reshape;reshape | solution.py:260
  96.8 6.7 reshape.799
  109.7 10.4 %select_reduce_fusion = (f32[6,1024]{1,0:T(8,128)S(1)}, f32[6,1024,1024]{1,2,0:T(8,128)}) fusion(pred[1024,1024]{0,1:T(8,128)(4,1)S(1)} %fusion.17, bf16[1024,6,64]{0,2,1:T(8,128)(2,1)S(1)} %bitcast.617, f32[1024,6,64]{0,2,1:T(8,128)S(1)} %bitcast.607, f32[6,64]{1,0:T(8,128)S(1)} %add.433), kind=kOutput, calls=%fused_computation.5 | convolution fusion | flops 819062784 | bytes 28599808 | tf_op jit(solution)/shard_map/qhd,khd->hqk/dot_general | solution.py:154
  120.1 10.9 %fusion = f32[6,1024]{1,0:T(8,128)S(1)} fusion(f32[6,1024,1024]{1,2,0:T(8,128)} %get-tuple-element.264, f32[6,1024]{1,0:T(8,128)S(1)} %get-tuple-element.263, pred[1024,1024]{0,1:T(8,128)(4,1)S(1)} %fusion.17), kind=kLoop, calls=%fused_computation.6 | loop fusion | flops 18868224 | bytes 26263552 | tf_op jit(solution)/shard_map/reduce_sum | solution.py:160
  131.0 12.2 %fusion.79 = bf16[6,64,1024]{2,1,0:T(8,128)(2,1)S(1)} fusion(f32[6,1024,1024]{1,2,0:T(8,128)} %get-tuple-element.264, f32[6,1024]{1,0:T(8,128)S(1)} %fusion, f32[6,1024]{1,0:T(8,128)S(1)} %get-tuple-element.263, pred[1024,1024]{0,1:T(8,128)(4,1)S(1)} %fusion.17, f32[1024,6,64]{0,2,1:T(8,128)S(1)} %bitcast.627, f32[6,64]{1,0:T(8,128)S(1)} %copy-done.73), kind=kOutput, calls=%fused_computation.133 | convolution fusion | flops 831651840 | bytes 28624384 | tf_op jit(solution)/shard_map/hqk,khd->qhd/dot_general | solution.py:162
  155.7 11.8 %collective-permute-done.25 = bf16[2,4,48,768]{3,2,1,0:T(8,128)(2,1)} collective-permute-done((bf16[2,4,48,768]{3,2,1,0:T(8,128)(2,1)}, bf16[2,4,48,768]{3,2,1,0:T(8,128)(2,1)}, u32[]{:S(2)}, u32[]{:S(2)}) %collective-permute-start.25) | collective-permute-done | bytes 589856 | tf_op jit(solution)/shard_map/ppermute | solution.py:30
  182.7 5.2 convolution_convert_fusion.3
  187.9 7.1 convert_reduce_fusion
  195.0 5.1 convolution_convert_fusion
  219.1 11.7 %collective-permute-done.53 = bf16[2,4,48,768]{3,2,1,0:T(8,128)(2,1)S(1)} collective-permute-done((bf16[2,4,48,768]{3,2,1,0:T(8,128)(2,1)S(1)}, bf16[2,4,48,768]{3,2,1,0:T(8,128)(2,1)S(1)}, u32[]{:S(2)}, u32[]{:S(2)}) %collective-permute-start.53) | collective-permute-done | bytes 589856 | tf_op jit(solution)/shard_map/ppermute | solution.py:30
  233.1 9.1 %collective-permute-done.45 = bf16[2,4,48,768]{3,2,1,0:T(8,128)(2,1)S(1)} collective-permute-done((bf16[2,4,48,768]{3,2,1,0:T(8,128)(2,1)S(1)}, bf16[2,4,48,768]{3,2,1,0:T(8,128)(2,1)S(1)}, u32[]{:S(2)}, u32[]{:S(2)}) %collective-permute-start.45) | collective-permute-done | bytes 589856 | tf_op jit(solution)/shard_map/ppermute | solution.py:30
  245.7 5.6 collective-permute-done.54
  289.5 12.2 %convert_reduce_fusion.4 = (f32[6,64]{1,0:T(8,128)}, bf16[6,64,1024]{2,1,0:T(8,128)(2,1)}) fusion(bf16[1024,6,64]{0,2,1:T(8,128)(2,1)S(1)} %bitcast.648, f32[6,1024,1024]{1,2,0:T(8,128)} %get-tuple-element.264, f32[6,1024]{1,0:T(8,128)S(1)} %copy-done.45, pred[1024,1024]{0,1:T(8,128)(4,1)S(1)} %copy-done.1), kind=kOutput, calls=%fused_computation.121 | convolution fusion | flops 825360000 | bytes 27813376 | tf_op jit(solution)/shard_map/hqk,qhd->khd/dot_general | solution.py:173
  301.7 21.3 %multiply_reduce_fusion = (f32[6,1024]{1,0:T(8,128)}, f32[6,1024,1024]{1,2,0:T(8,128)}) fusion(f32[6,1024,1024]{1,2,0:T(8,128)} %get-tuple-element.264, f32[6,1024]{1,0:T(8,128)} %log_add_fusion, pred[1024,1024]{0,1:T(8,128)(4,1)S(1)} %copy-done.1, bf16[1024,6,64]{0,2,1:T(8,128)(2,1)S(1)} %bitcast.649, f32[1024,6,64]{0,2,1:T(8,128)S(1)} %bitcast.628, ...), kind=kOutput, calls=%fused_computation.1 | convolution fusion | flops 831252480 | bytes 53790208 | tf_op jit(solution)/shard_map/qhd,khd->hqk/dot_general | solution.py:176
  323.0 18.2 %multiply_convert_fusion = bf16[6,1024,1024]{1,2,0:T(8,128)(2,1)S(1)} fusion(f32[6,1024,1024]{1,2,0:T(8,128)} %get-tuple-element.266, f32[6,1024,1024]{1,2,0:T(8,128)} %get-tuple-element.264, f32[6,1024]{1,0:T(8,128)} %get-tuple-element.265, f32[6,1024]{1,0:T(8,128)} %log_add_fusion, pred[1024,1024]{0,1:T(8,128)(4,1)} %copy-done), kind=kLoop, calls=%fused_computation | loop fusion | flops 31457280 | bytes 64012288 | tf_op jit(solution)/shard_map/convert_element_type | solution.py:178
  341.3 6.3 convolution_convert_fusion.4
  347.5 4.9 convert_reduce_fusion.5
  353.8 4.4 convert_bitcast_fusion
  361.8 6.1 concatenate.52
  376.5 8.1 %collective-permute-done.33 = bf16[4,2,48,768]{3,2,1,0:T(8,128)(2,1)S(1)} collective-permute-done((bf16[4,2,48,768]{3,2,1,0:T(8,128)(2,1)S(1)}, bf16[4,2,48,768]{3,2,1,0:T(8,128)(2,1)S(1)}, u32[]{:S(2)}, u32[]{:S(2)}) %collective-permute-start.33) | collective-permute-done | bytes 589856 | tf_op jit(solution)/shard_map/ppermute | solution.py:30
  391.9 13.0 %collective-permute-done.38 = bf16[4,48,768]{2,1,0:T(8,128)(2,1)S(1)} collective-permute-done((bf16[4,48,768]{2,1,0:T(8,128)(2,1)S(1)}, bf16[4,48,768]{2,1,0:T(8,128)(2,1)S(1)}, u32[]{:S(2)}, u32[]{:S(2)}) %collective-permute-start.38) | collective-permute-done | bytes 294944 | tf_op jit(solution)/shard_map/ppermute | solution.py:30
  421.9 6.5 all-to-all-start
  442.7 11.7 %all-to-all-done = bf16[8,96,768]{2,1,0:T(8,128)(2,1)} async-done(((bf16[8,96,768]{2,1,0:T(8,128)(2,1)}), bf16[8,96,768]{2,1,0:T(8,128)(2,1)}, u32[]{:S(2)}, u32[]{:S(2)}) %all-to-all-start) | async-done | bytes 1179680 | tf_op jit(solution)/shard_map/all_to_all | solution.py:382
  459.8 5.1 add_convert_fusion
  464.9 74.3 %psum.7 = f32[6912]{0:T(1024)S(1)} all-reduce(f32[6912]{0:T(1024)S(1)} %pad_maximum_fusion.47), channel_id=1, replica_groups=mesh['z'=4,'y'=2,'x'=2,'c'=2] {'z','y','x'}, use_global_device_ids=true, to_apply=%region_24.25 | all-reduce | flops 6912 | bytes 55296 | tf_op jit(solution)/shard_map/psum | solution.py:347
  547.2 16.9 %collective-permute-done.58 = f32[384,768]{1,0:T(8,128)S(1)} collective-permute-done((f32[384,768]{1,0:T(8,128)S(1)}, f32[384,768]{1,0:T(8,128)S(1)}, u32[]{:S(2)}, u32[]{:S(2)}) %collective-permute-start.58) | collective-permute-done | bytes 1179680 | tf_op jit(solution)/shard_map/ppermute | solution.py:30
  575.1 6.0 fusion.264
  581.0 6.5 fusion.64
  587.6 6.1 fusion.62
  593.7 6.1 fusion.265
  599.8 6.3 fusion.55
  606.2 6.1 fusion.59
  612.3 6.3 fusion.57
  618.6 6.0 fusion.266
  624.6 6.6 fusion.53
  631.2 6.1 fusion.49
  637.3 6.3 fusion.51
  643.6 6.0 fusion.267
  649.6 6.4 fusion.47
  655.9 6.1 fusion.43
  662.1 6.1 fusion.45
  668.2 6.4 fusion.268
  674.6 6.1 fusion.32
  680.7 8.3 %fusion.71 = bf16[768,768]{1,0:T(8,128)(2,1)} fusion(f32[768,768]{1,0:T(8,128)S(1)} %fusion.32, bf16[768,768]{1,0:T(8,128)(2,1)} %bitcast.198, f32[]{:T(128)S(6)} %div.117), kind=kOutput, calls=%fused_computation.127 | convolution fusion | flops 5437587456 | bytes 4718596 | tf_op jit(solution)/shard_map/dot_general | solution.py:123
  700.6 21.6 %all-to-all-done.1 = bf16[8,96,768]{2,1,0:T(8,128)(2,1)S(1)} async-done(((bf16[8,96,768]{2,1,0:T(8,128)(2,1)}), bf16[8,96,768]{2,1,0:T(8,128)(2,1)S(1)}, u32[]{:S(2)}, u32[]{:S(2)}) %all-to-all-start.1) | async-done | bytes 1179680 | tf_op jit(solution)/shard_map/all_to_all | solution.py:384
  (526 shorter events, 255.0 us)
Async XLA Ops:
  4.2 27.0 %collective-permute-start.8 = (f32[1152]{0:T(1024)}, f32[1152]{0:T(1024)}, u32[]{:S(2)}, u32[]{:S(2)}) collective-permute-start(f32[1152]{0:T(1024)} %constant_dynamic-update-slice_fusion.3), channel_id=1, source_target_pairs={{0,2},{2,0},{1,3},{3,1},{4,6},{6,4},{5,7},{7,5},{8,10},{10,8},{9,1... | collective-permute-start | bytes 13832 | tf_op jit(solution)/shard_map/ppermute | solution.py:30
  8.7 29.8 %collective-permute-start.18 = (bf16[48,768]{1,0:T(8,128)(2,1)}, bf16[48,768]{1,0:T(8,128)(2,1)}, u32[]{:S(2)}, u32[]{:S(2)}) collective-permute-start(bf16[48,768]{1,0:T(8,128)(2,1)} %slice.630), channel_id=1, source_target_pairs={{0,16},{8,24},{16,0},{24,8},{1,17},{9,25},{17,1},{25,9},{2,18},{10... | collective-permute-start | bytes 221192 | tf_op jit(solution)/shard_map/ppermute | solution.py:30
  12.4 23.0 %collective-permute-start = (bf16[48,576]{1,0:T(8,128)(2,1)S(1)}, bf16[48,576]{1,0:T(8,128)(2,1)}, u32[]{:S(2)}, u32[]{:S(2)}) collective-permute-start(bf16[48,576]{1,0:T(8,128)(2,1)S(1)} %slice.511), channel_id=1, source_target_pairs={{0,16},{8,24},{16,0},{24,8},{1,17},{9,25},{17,1},{25,9},{2,18},{10... | collective-permute-start | bytes 165896 | tf_op jit(solution)/shard_map/ppermute | solution.py:30
  13.6 21.8 %collective-permute-start.4 = (bf16[48,576]{1,0:T(8,128)(2,1)}, bf16[48,576]{1,0:T(8,128)(2,1)}, u32[]{:S(2)}, u32[]{:S(2)}) collective-permute-start(bf16[48,576]{1,0:T(8,128)(2,1)} %slice.513), channel_id=1, source_target_pairs={{0,16},{8,24},{16,0},{24,8},{1,17},{9,25},{17,1},{25,9},{2,18},{10... | collective-permute-start | bytes 165896 | tf_op jit(solution)/shard_map/ppermute | solution.py:30
  18.1 21.7 %collective-permute-start.9 = (bf16[48,960]{1,0:T(8,128)(2,1)S(1)}, bf16[48,960]{1,0:T(8,128)(2,1)}, u32[]{:S(2)}, u32[]{:S(2)}) collective-permute-start(bf16[48,960]{1,0:T(8,128)(2,1)S(1)} %get-tuple-element.244), channel_id=1, source_target_pairs={{0,16},{8,24},{16,0},{24,8},{1,17},{9,25},{17,1},{25,9},{2,18},{10... | collective-permute-start | bytes 276488 | tf_op jit(solution)/shard_map/ppermute | solution.py:30
  31.2 11.2 %collective-permute-start.13 = (bf16[48,960]{1,0:T(8,128)(2,1)S(1)}, bf16[48,960]{1,0:T(8,128)(2,1)S(1)}, u32[]{:S(2)}, u32[]{:S(2)}) collective-permute-start(bf16[48,960]{1,0:T(8,128)(2,1)S(1)} %get-tuple-element.245), channel_id=1, source_target_pairs={{0,16},{8,24},{16,0},{24,8},{1,17},{9,25},{17,1},{25,9},{2,18},{10... | collective-permute-start | bytes 276488 | tf_op jit(solution)/shard_map/ppermute | solution.py:30
  36.3 10.9 %collective-permute-start.1 = (bf16[2,48,576]{2,1,0:T(8,128)(2,1)S(1)}, bf16[2,48,576]{2,1,0:T(8,128)(2,1)S(1)}, u32[]{:S(2)}, u32[]{:S(2)}) collective-permute-start(bf16[2,48,576]{2,1,0:T(8,128)(2,1)S(1)} %pad_maximum_fusion.43), channel_id=1, source_target_pairs={{0,8},{8,0},{16,24},{24,16},{1,9},{9,1},{17,25},{25,17},{2,10},{10... | collective-permute-start | bytes 331784 | tf_op jit(solution)/shard_map/ppermute | solution.py:30
  38.0 10.2 %collective-permute-start.5 = (bf16[2,48,576]{2,1,0:T(8,128)(2,1)S(1)}, bf16[2,48,576]{2,1,0:T(8,128)(2,1)S(1)}, u32[]{:S(2)}, u32[]{:S(2)}) collective-permute-start(bf16[2,48,576]{2,1,0:T(8,128)(2,1)S(1)} %pad_maximum_fusion.44), channel_id=1, source_target_pairs={{0,8},{8,0},{16,24},{24,16},{1,9},{9,1},{17,25},{25,17},{2,10},{10... | collective-permute-start | bytes 331784 | tf_op jit(solution)/shard_map/ppermute | solution.py:30
  39.8 10.2 %collective-permute-start.19 = (bf16[2,48,768]{2,1,0:T(8,128)(2,1)S(1)}, bf16[2,48,768]{2,1,0:T(8,128)(2,1)S(1)}, u32[]{:S(2)}, u32[]{:S(2)}) collective-permute-start(bf16[2,48,768]{2,1,0:T(8,128)(2,1)S(1)} %pad_maximum_fusion.41), channel_id=1, source_target_pairs={{0,8},{8,0},{16,24},{24,16},{1,9},{9,1},{17,25},{25,17},{2,10},{10... | collective-permute-start | bytes 442376 | tf_op jit(solution)/shard_map/ppermute | solution.py:30
  42.4 16.4 %collective-permute-start.10 = (bf16[2,48,960]{2,1,0:T(8,128)(2,1)S(1)}, bf16[2,48,960]{2,1,0:T(8,128)(2,1)S(1)}, u32[]{:S(2)}, u32[]{:S(2)}) collective-permute-start(bf16[2,48,960]{2,1,0:T(8,128)(2,1)S(1)} %pad_maximum_fusion.39), channel_id=1, source_target_pairs={{0,8},{8,0},{16,24},{24,16},{1,9},{9,1},{17,25},{25,17},{2,10},{10... | collective-permute-start | bytes 552968 | tf_op jit(solution)/shard_map/ppermute | solution.py:30
  46.0 11.3 %collective-permute-start.14 = (bf16[2,48,960]{2,1,0:T(8,128)(2,1)S(1)}, bf16[2,48,960]{2,1,0:T(8,128)(2,1)S(1)}, u32[]{:S(2)}, u32[]{:S(2)}) collective-permute-start(bf16[2,48,960]{2,1,0:T(8,128)(2,1)S(1)} %pad_maximum_fusion.40), channel_id=1, source_target_pairs={{0,8},{8,0},{16,24},{24,16},{1,9},{9,1},{17,25},{25,17},{2,10},{10... | collective-permute-start | bytes 552968 | tf_op jit(solution)/shard_map/ppermute | solution.py:30
  47.2 12.3 %collective-permute-start.23 = (bf16[2,48,768]{2,1,0:T(8,128)(2,1)S(1)}, bf16[2,48,768]{2,1,0:T(8,128)(2,1)S(1)}, u32[]{:S(2)}, u32[]{:S(2)}) collective-permute-start(bf16[2,48,768]{2,1,0:T(8,128)(2,1)S(1)} %pad_maximum_fusion.42), channel_id=1, source_target_pairs={{0,8},{8,0},{16,24},{24,16},{1,9},{9,1},{17,25},{25,17},{2,10},{10... | collective-permute-start | bytes 442376 | tf_op jit(solution)/shard_map/ppermute | solution.py:30
  48.4 14.2 %collective-permute-start.6 = (bf16[4,48,576]{2,1,0:T(8,128)(2,1)S(1)}, bf16[4,48,576]{2,1,0:T(8,128)(2,1)S(1)}, u32[]{:S(2)}, u32[]{:S(2)}) collective-permute-start(bf16[4,48,576]{2,1,0:T(8,128)(2,1)S(1)} %bitcast.650), channel_id=1, source_target_pairs={{0,2},{2,0},{1,3},{3,1},{4,6},{6,4},{5,7},{7,5},{8,10},{10,8},{9,1... | collective-permute-start | bytes 663560 | tf_op jit(solution)/shard_map/ppermute | solution.py:30
  50.0 11.1 %collective-permute-start.2 = (bf16[4,48,576]{2,1,0:T(8,128)(2,1)S(1)}, bf16[4,48,576]{2,1,0:T(8,128)(2,1)S(1)}, u32[]{:S(2)}, u32[]{:S(2)}) collective-permute-start(bf16[4,48,576]{2,1,0:T(8,128)(2,1)S(1)} %bitcast.665), channel_id=1, source_target_pairs={{0,4},{4,0},{1,5},{5,1},{2,6},{6,2},{3,7},{7,3},{8,12},{12,8},{9,1... | collective-permute-start | bytes 663560 | tf_op jit(solution)/shard_map/ppermute | solution.py:30
  57.2 9.9 %collective-permute-start.20 = (bf16[4,48,768]{2,1,0:T(8,128)(2,1)S(1)}, bf16[4,48,768]{2,1,0:T(8,128)(2,1)S(1)}, u32[]{:S(2)}, u32[]{:S(2)}) collective-permute-start(bf16[4,48,768]{2,1,0:T(8,128)(2,1)S(1)} %bitcast.664), channel_id=1, source_target_pairs={{0,4},{4,0},{1,5},{5,1},{2,6},{6,2},{3,7},{7,3},{8,12},{12,8},{9,1... | collective-permute-start | bytes 884744 | tf_op jit(solution)/shard_map/ppermute | solution.py:30
  58.9 18.6 %collective-permute-start.15 = (bf16[4,48,960]{2,1,0:T(8,128)(2,1)S(1)}, bf16[4,48,960]{2,1,0:T(8,128)(2,1)S(1)}, u32[]{:S(2)}, u32[]{:S(2)}) collective-permute-start(bf16[4,48,960]{2,1,0:T(8,128)(2,1)S(1)} %bitcast.645), channel_id=1, source_target_pairs={{0,2},{2,0},{1,3},{3,1},{4,6},{6,4},{5,7},{7,5},{8,10},{10,8},{9,1... | collective-permute-start | bytes 1105928 | tf_op jit(solution)/shard_map/ppermute | solution.py:30
  59.6 16.0 %collective-permute-start.11 = (bf16[4,48,960]{2,1,0:T(8,128)(2,1)S(1)}, bf16[4,48,960]{2,1,0:T(8,128)(2,1)S(1)}, u32[]{:S(2)}, u32[]{:S(2)}) collective-permute-start(bf16[4,48,960]{2,1,0:T(8,128)(2,1)S(1)} %bitcast.654), channel_id=1, source_target_pairs={{0,4},{4,0},{1,5},{5,1},{2,6},{6,2},{3,7},{7,3},{8,12},{12,8},{9,1... | collective-permute-start | bytes 1105928 | tf_op jit(solution)/shard_map/ppermute | solution.py:30
  61.1 88.3 %collective-permute-start.24 = (bf16[4,48,768]{2,1,0:T(8,128)(2,1)}, bf16[4,48,768]{2,1,0:T(8,128)(2,1)}, u32[]{:S(2)}, u32[]{:S(2)}) collective-permute-start(bf16[4,48,768]{2,1,0:T(8,128)(2,1)} %bitcast.73), channel_id=1, source_target_pairs={{0,2},{2,0},{1,3},{3,1},{4,6},{6,4},{5,7},{7,5},{8,10},{10,8},{9,1... | collective-permute-start | bytes 884744 | tf_op jit(solution)/shard_map/ppermute | solution.py:30
  62.6 25.2 %collective-permute-start.3 = (bf16[4,2,48,576]{3,2,0,1:T(8,128)(2,1)S(1)}, bf16[4,2,48,576]{3,2,0,1:T(8,128)(2,1)S(1)}, u32[]{:S(2)}, u32[]{:S(2)}) collective-permute-start(bf16[4,2,48,576]{3,2,0,1:T(8,128)(2,1)S(1)} %get-tuple-element.221), channel_id=1, source_target_pairs={{0,2},{2,0},{1,3},{3,1},{4,6},{6,4},{5,7},{7,5},{8,10},{10,8},{9,1... | collective-permute-start | bytes 1327112 | tf_op jit(solution)/shard_map/ppermute | solution.py:30
  67.2 21.3 %collective-permute-start.7 = (bf16[2,4,48,576]{3,2,1,0:T(8,128)(2,1)S(1)}, bf16[2,4,48,576]{3,2,1,0:T(8,128)(2,1)S(1)}, u32[]{:S(2)}, u32[]{:S(2)}) collective-permute-start(bf16[2,4,48,576]{3,2,1,0:T(8,128)(2,1)S(1)} %pad_maximum_fusion.29), channel_id=1, source_target_pairs={{0,4},{4,0},{1,5},{5,1},{2,6},{6,2},{3,7},{7,3},{8,12},{12,8},{9,1... | collective-permute-start | bytes 1327112 | tf_op jit(solution)/shard_map/ppermute | solution.py:30
  75.6 78.7 %collective-permute-start.21 = (bf16[4,2,48,768]{3,2,0,1:T(8,128)(2,1)}, bf16[4,2,48,768]{3,2,0,1:T(8,128)(2,1)}, u32[]{:S(2)}, u32[]{:S(2)}) collective-permute-start(bf16[4,2,48,768]{3,2,0,1:T(8,128)(2,1)} %get-tuple-element.217), channel_id=1, source_target_pairs={{0,2},{2,0},{1,3},{3,1},{4,6},{6,4},{5,7},{7,5},{8,10},{10,8},{9,1... | collective-permute-start | bytes 1769480 | tf_op jit(solution)/shard_map/ppermute | solution.py:30
  77.5 67.3 %collective-permute-start.12 = (bf16[4,2,48,960]{3,2,0,1:T(8,128)(2,1)}, bf16[4,2,48,960]{3,2,0,1:T(8,128)(2,1)}, u32[]{:S(2)}, u32[]{:S(2)}) collective-permute-start(bf16[4,2,48,960]{3,2,0,1:T(8,128)(2,1)} %get-tuple-element.207), channel_id=1, source_target_pairs={{0,2},{2,0},{1,3},{3,1},{4,6},{6,4},{5,7},{7,5},{8,10},{10,8},{9,1... | collective-permute-start | bytes 2211848 | tf_op jit(solution)/shard_map/ppermute | solution.py:30
  87.8 55.4 %collective-permute-start.16 = (bf16[2,4,48,960]{3,2,1,0:T(8,128)(2,1)}, bf16[2,4,48,960]{3,2,1,0:T(8,128)(2,1)}, u32[]{:S(2)}, u32[]{:S(2)}) collective-permute-start(bf16[2,4,48,960]{3,2,1,0:T(8,128)(2,1)} %pad_maximum_fusion.25), channel_id=1, source_target_pairs={{0,4},{4,0},{1,5},{5,1},{2,6},{6,2},{3,7},{7,3},{8,12},{12,8},{9,1... | collective-permute-start | bytes 2211848 | tf_op jit(solution)/shard_map/ppermute | solution.py:30
  149.5 26.5 %collective-permute-start.17 = (bf16[1024,768]{1,0:T(8,128)(2,1)}, bf16[1024,768]{1,0:T(8,128)(2,1)}, u32[]{:S(2)}, u32[]{:S(2)}) collective-permute-start(bf16[1024,768]{1,0:T(8,128)(2,1)} %bitcast_convert_fusion.3), channel_id=1, source_target_pairs={{0,1},{1,0},{2,3},{3,2},{4,5},{5,4},{6,7},{7,6},{8,9},{9,8},{10,11... | collective-permute-start | bytes 4718600 | tf_op jit(solution)/shard_map/ppermute | solution.py:30
  151.4 16.1 %collective-permute-start.25 = (bf16[2,4,48,768]{3,2,1,0:T(8,128)(2,1)}, bf16[2,4,48,768]{3,2,1,0:T(8,128)(2,1)}, u32[]{:S(2)}, u32[]{:S(2)}) collective-permute-start(bf16[2,4,48,768]{3,2,1,0:T(8,128)(2,1)} %pad_maximum_fusion.27), channel_id=1, source_target_pairs={{0,4},{4,0},{1,5},{5,1},{2,6},{6,2},{3,7},{7,3},{8,12},{12,8},{9,1... | collective-permute-start | bytes 1769480 | tf_op jit(solution)/shard_map/ppermute | solution.py:30
  214.5 16.3 %collective-permute-start.53 = (bf16[2,4,48,768]{3,2,1,0:T(8,128)(2,1)S(1)}, bf16[2,4,48,768]{3,2,1,0:T(8,128)(2,1)S(1)}, u32[]{:S(2)}, u32[]{:S(2)}) collective-permute-start(bf16[2,4,48,768]{3,2,1,0:T(8,128)(2,1)S(1)} %select_bitcast_fusion.8), channel_id=1, source_target_pairs={{0,4},{4,0},{1,5},{5,1},{2,6},{6,2},{3,7},{7,3},{8,12},{12,8},{9,1... | collective-permute-start | bytes 1769480 | tf_op jit(solution)/shard_map/ppermute | solution.py:30
  216.1 16.3 %collective-permute-start.49 = (bf16[4,2,48,768]{3,2,0,1:T(8,128)(2,1)S(1)}, bf16[4,2,48,768]{3,2,0,1:T(8,128)(2,1)S(1)}, u32[]{:S(2)}, u32[]{:S(2)}) collective-permute-start(bf16[4,2,48,768]{3,2,0,1:T(8,128)(2,1)S(1)} %copy_bitcast_fusion.6), channel_id=1, source_target_pairs={{0,2},{2,0},{1,3},{3,1},{4,6},{6,4},{5,7},{7,5},{8,10},{10,8},{9,1... | collective-permute-start | bytes 1769480 | tf_op jit(solution)/shard_map/ppermute | solution.py:30
  216.6 62.0 %collective-permute-start.29 = (bf16[1024,768]{1,0:T(8,128)(2,1)S(1)}, bf16[1024,768]{1,0:T(8,128)(2,1)S(1)}, u32[]{:S(2)}, u32[]{:S(2)}) collective-permute-start(bf16[1024,768]{1,0:T(8,128)(2,1)S(1)} %copy-done.16), channel_id=1, source_target_pairs={{0,1},{1,0},{2,3},{3,2},{4,5},{5,4},{6,7},{7,6},{8,9},{9,8},{10,11... | collective-permute-start | bytes 4718600 | tf_op jit(solution)/shard_map/ppermute | solution.py:30
  217.0 25.1 %collective-permute-start.45 = (bf16[2,4,48,768]{3,2,1,0:T(8,128)(2,1)S(1)}, bf16[2,4,48,768]{3,2,1,0:T(8,128)(2,1)S(1)}, u32[]{:S(2)}, u32[]{:S(2)}) collective-permute-start(bf16[2,4,48,768]{3,2,1,0:T(8,128)(2,1)S(1)} %select_bitcast_fusion.9), channel_id=1, source_target_pairs={{0,4},{4,0},{1,5},{5,1},{2,6},{6,2},{3,7},{7,3},{8,12},{12,8},{9,1... | collective-permute-start | bytes 1769480 | tf_op jit(solution)/shard_map/ppermute | solution.py:30
  217.6 27.4 %collective-permute-start.41 = (bf16[4,2,48,768]{3,2,0,1:T(8,128)(2,1)S(1)}, bf16[4,2,48,768]{3,2,0,1:T(8,128)(2,1)S(1)}, u32[]{:S(2)}, u32[]{:S(2)}) collective-permute-start(bf16[4,2,48,768]{3,2,0,1:T(8,128)(2,1)S(1)} %copy_bitcast_fusion.8), channel_id=1, source_target_pairs={{0,2},{2,0},{1,3},{3,1},{4,6},{6,4},{5,7},{7,5},{8,10},{10,8},{9,1... | collective-permute-start | bytes 1769480 | tf_op jit(solution)/shard_map/ppermute | solution.py:30
  230.8 50.3 %collective-permute-start.26 = (bf16[1024,768]{1,0:T(8,128)(2,1)S(1)}, bf16[1024,768]{1,0:T(8,128)(2,1)S(1)}, u32[]{:S(2)}, u32[]{:S(2)}) collective-permute-start(bf16[1024,768]{1,0:T(8,128)(2,1)S(1)} %copy-done.25), channel_id=1, source_target_pairs={{0,1},{1,0},{2,3},{3,2},{4,5},{5,4},{6,7},{7,6},{8,9},{9,8},{10,11... | collective-permute-start | bytes 4718600 | tf_op jit(solution)/shard_map/ppermute | solution.py:30
  232.4 19.0 %collective-permute-start.54 = (bf16[4,48,768]{2,1,0:T(8,128)(2,1)S(1)}, bf16[4,48,768]{2,1,0:T(8,128)(2,1)S(1)}, u32[]{:S(2)}, u32[]{:S(2)}) collective-permute-start(bf16[4,48,768]{2,1,0:T(8,128)(2,1)S(1)} %fusion.152), channel_id=1, source_target_pairs={{0,2},{2,0},{1,3},{3,1},{4,6},{6,4},{5,7},{7,5},{8,10},{10,8},{9,1... | collective-permute-start | bytes 884744 | tf_op jit(solution)/shard_map/ppermute | solution.py:30
  242.2 9.8 %collective-permute-start.50 = (bf16[4,48,768]{2,1,0:T(8,128)(2,1)S(1)}, bf16[4,48,768]{2,1,0:T(8,128)(2,1)S(1)}, u32[]{:S(2)}, u32[]{:S(2)}) collective-permute-start(bf16[4,48,768]{2,1,0:T(8,128)(2,1)S(1)} %fusion.149), channel_id=1, source_target_pairs={{0,4},{4,0},{1,5},{5,1},{2,6},{6,2},{3,7},{7,3},{8,12},{12,8},{9,1... | collective-permute-start | bytes 884744 | tf_op jit(solution)/shard_map/ppermute | solution.py:30
  245.0 11.1 %collective-permute-start.46 = (bf16[4,48,768]{2,1,0:T(8,128)(2,1)S(1)}, bf16[4,48,768]{2,1,0:T(8,128)(2,1)S(1)}, u32[]{:S(2)}, u32[]{:S(2)}) collective-permute-start(bf16[4,48,768]{2,1,0:T(8,128)(2,1)S(1)} %fusion.151), channel_id=1, source_target_pairs={{0,2},{2,0},{1,3},{3,1},{4,6},{6,4},{5,7},{7,5},{8,10},{10,8},{9,1... | collective-permute-start | bytes 884744 | tf_op jit(solution)/shard_map/ppermute | solution.py:30
  259.7 8.7 %collective-permute-start.43 = (bf16[2,48,768]{2,1,0:T(8,128)(2,1)S(1)}, bf16[2,48,768]{2,1,0:T(8,128)(2,1)S(1)}, u32[]{:S(2)}, u32[]{:S(2)}) collective-permute-start(bf16[2,48,768]{2,1,0:T(8,128)(2,1)S(1)} %fusion.162), channel_id=1, source_target_pairs={{0,8},{8,0},{16,24},{24,16},{1,9},{9,1},{17,25},{25,17},{2,10},{10... | collective-permute-start | bytes 442376 | tf_op jit(solution)/shard_map/ppermute | solution.py:30
  368.2 16.3 %collective-permute-start.33 = (bf16[4,2,48,768]{3,2,1,0:T(8,128)(2,1)S(1)}, bf16[4,2,48,768]{3,2,1,0:T(8,128)(2,1)S(1)}, u32[]{:S(2)}, u32[]{:S(2)}) collective-permute-start(bf16[4,2,48,768]{3,2,1,0:T(8,128)(2,1)S(1)} %maximum_bitcast_fusion.2), channel_id=1, source_target_pairs={{0,2},{2,0},{1,3},{3,1},{4,6},{6,4},{5,7},{7,5},{8,10},{10,8},{9,1... | collective-permute-start | bytes 1769480 | tf_op jit(solution)/shard_map/ppermute | solution.py:30
  368.9 17.5 %collective-permute-start.37 = (bf16[2,4,48,768]{3,2,1,0:T(8,128)(2,1)S(1)}, bf16[2,4,48,768]{3,2,1,0:T(8,128)(2,1)S(1)}, u32[]{:S(2)}, u32[]{:S(2)}) collective-permute-start(bf16[2,4,48,768]{3,2,1,0:T(8,128)(2,1)S(1)} %fusion.137), channel_id=1, source_target_pairs={{0,4},{4,0},{1,5},{5,1},{2,6},{6,2},{3,7},{7,3},{8,12},{12,8},{9,1... | collective-permute-start | bytes 1769480 | tf_op jit(solution)/shard_map/ppermute | solution.py:30
  375.0 58.8 %collective-permute-start.27 = (bf16[512,768]{1,0:T(8,128)(2,1)}, bf16[512,768]{1,0:T(8,128)(2,1)}, u32[]{:S(2)}, u32[]{:S(2)}) collective-permute-start(bf16[512,768]{1,0:T(8,128)(2,1)} %constant_dynamic-slice_fusion.2), channel_id=1, source_target_pairs={{0,2},{2,0},{1,3},{3,1},{4,6},{6,4},{5,7},{7,5},{8,10},{10,8},{9,1... | collective-permute-start | bytes 2359304 | tf_op jit(solution)/shard_map/ppermute | solution.py:30
  376.5 59.9 %collective-permute-start.30 = (bf16[1024,768]{1,0:T(8,128)(2,1)}, bf16[1024,768]{1,0:T(8,128)(2,1)}, u32[]{:S(2)}, u32[]{:S(2)}) collective-permute-start(bf16[1024,768]{1,0:T(8,128)(2,1)} %bitcast_convert_fusion.1), channel_id=1, source_target_pairs={{0,1},{1,0},{2,3},{3,2},{4,5},{5,4},{6,7},{7,6},{8,9},{9,8},{10,11... | collective-permute-start | bytes 4718600 | tf_op jit(solution)/shard_map/ppermute | solution.py:30
  386.7 18.3 %collective-permute-start.38 = (bf16[4,48,768]{2,1,0:T(8,128)(2,1)S(1)}, bf16[4,48,768]{2,1,0:T(8,128)(2,1)S(1)}, u32[]{:S(2)}, u32[]{:S(2)}) collective-permute-start(bf16[4,48,768]{2,1,0:T(8,128)(2,1)S(1)} %fusion.150), channel_id=1, source_target_pairs={{0,2},{2,0},{1,3},{3,1},{4,6},{6,4},{5,7},{7,5},{8,10},{10,8},{9,1... | collective-permute-start | bytes 884744 | tf_op jit(solution)/shard_map/ppermute | solution.py:30
  391.7 13.5 %collective-permute-start.35 = (bf16[2,48,768]{2,1,0:T(8,128)(2,1)S(1)}, bf16[2,48,768]{2,1,0:T(8,128)(2,1)S(1)}, u32[]{:S(2)}, u32[]{:S(2)}) collective-permute-start(bf16[2,48,768]{2,1,0:T(8,128)(2,1)S(1)} %fusion.160), channel_id=1, source_target_pairs={{0,8},{8,0},{16,24},{24,16},{1,9},{9,1},{17,25},{25,17},{2,10},{10... | collective-permute-start | bytes 442376 | tf_op jit(solution)/shard_map/ppermute | solution.py:30
  421.9 32.5 %all-to-all-start = ((bf16[8,96,768]{2,1,0:T(8,128)(2,1)}), bf16[8,96,768]{2,1,0:T(8,128)(2,1)}, u32[]{:S(2)}, u32[]{:S(2)}) async-start(bf16[8,96,768]{2,1,0:T(8,128)(2,1)} %fusion.169), calls=%async_computation | async-start | bytes 2359296 | tf_op jit(solution)/shard_map/all_to_all | solution.py:382
  433.8 110.2 %collective-permute-start.28 = (bf16[512,768]{1,0:T(8,128)(2,1)}, bf16[512,768]{1,0:T(8,128)(2,1)}, u32[]{:S(2)}, u32[]{:S(2)}) collective-permute-start(bf16[512,768]{1,0:T(8,128)(2,1)} %collective-permute-done.27), channel_id=1, source_target_pairs={{0,1},{1,0},{2,3},{3,2},{4,5},{5,4},{6,7},{7,6},{8,9},{9,8},{10,11... | collective-permute-start | bytes 2359304 | tf_op jit(solution)/shard_map/ppermute | solution.py:30
  459.7 79.7 %collective-permute-start.57 = (f32[384,768]{1,0:T(8,128)}, f32[384,768]{1,0:T(8,128)}, u32[]{:S(2)}, u32[]{:S(2)}) collective-permute-start(f32[384,768]{1,0:T(8,128)} %slice_select_fusion), channel_id=1, source_target_pairs={{0,1},{1,0},{2,3},{3,2},{4,5},{5,4},{6,7},{7,6},{8,9},{9,8},{10,11... | collective-permute-start | bytes 3538952 | tf_op jit(solution)/shard_map/ppermute | solution.py:30
  541.7 22.3 %collective-permute-start.58 = (f32[384,768]{1,0:T(8,128)S(1)}, f32[384,768]{1,0:T(8,128)S(1)}, u32[]{:S(2)}, u32[]{:S(2)}) collective-permute-start(f32[384,768]{1,0:T(8,128)S(1)} %select_add_fusion.5), channel_id=1, source_target_pairs={{0,2},{2,0},{1,3},{3,1},{4,6},{6,4},{5,7},{7,5},{8,10},{10,8},{9,1... | collective-permute-start | bytes 3538952 | tf_op jit(solution)/shard_map/ppermute | solution.py:30
  541.9 30.6 %collective-permute-start.31 = (bf16[512,768]{1,0:T(8,128)(2,1)S(1)}, bf16[512,768]{1,0:T(8,128)(2,1)S(1)}, u32[]{:S(2)}, u32[]{:S(2)}) collective-permute-start(bf16[512,768]{1,0:T(8,128)(2,1)S(1)} %constant_dynamic-slice_fusion.1), channel_id=1, source_target_pairs={{0,2},{2,0},{1,3},{3,1},{4,6},{6,4},{5,7},{7,5},{8,10},{10,8},{9,1... | collective-permute-start | bytes 2359304 | tf_op jit(solution)/shard_map/ppermute | solution.py:30
  572.5 121.5 %collective-permute-start.32 = (bf16[512,768]{1,0:T(8,128)(2,1)S(1)}, bf16[512,768]{1,0:T(8,128)(2,1)}, u32[]{:S(2)}, u32[]{:S(2)}) collective-permute-start(bf16[512,768]{1,0:T(8,128)(2,1)S(1)} %collective-permute-done.31), channel_id=1, source_target_pairs={{0,1},{1,0},{2,3},{3,2},{4,5},{5,4},{6,7},{7,6},{8,9},{9,8},{10,11... | collective-permute-start | bytes 2359304 | tf_op jit(solution)/shard_map/ppermute | solution.py:30
  689.0 33.2 %all-to-all-start.1 = ((bf16[8,96,768]{2,1,0:T(8,128)(2,1)}), bf16[8,96,768]{2,1,0:T(8,128)(2,1)S(1)}, u32[]{:S(2)}, u32[]{:S(2)}) async-start(bf16[8,96,768]{2,1,0:T(8,128)(2,1)} %bitcast.202), calls=%async_computation.1 | async-start | bytes 2359296 | tf_op jit(solution)/shard_map/all_to_all | solution.py:384
  (101 other events, 932.0 us)

commit v2 on v1

v2 whole, which is shorter than its diff:
```python
import math

import jax
import jax.numpy as jnp
from jax import lax
from jax.experimental import pallas as pl
from jax.experimental.pallas import tpu as pltpu
from jax.sharding import Mesh, PartitionSpec as P

D = 768
HEAD_DIM = 64
FF = 3072
SLOTS = 1024
NS_STEPS = 5

EPS = 1e-05
MOMENTUM = 0.9
NS_A = 3.4445
NS_B = -4.775
NS_C = 2.0315
RATE = 1.0
DECAY = 0.01
VECTOR_RATE = 0.1
FLOOR = -1e30
TILE = 256
ROWS = 256

BF = jnp.bfloat16
F32 = jnp.float32


def swap(value, axis, distance=1):
    size = lax.axis_size(axis)
    return lax.ppermute(value, axis, [(i, i ^ distance) for i in range(size)])


def join(mine, theirs, bit, dim):
    low = jnp.where(bit, theirs, mine)
    high = jnp.where(bit, mine, theirs)
    return jnp.stack((low, high), axis=dim)


def distances(axis):
    found = []
    step = lax.axis_size(axis) // 2
    while step >= 1:
        found.append(step)
        step //= 2
    return found


def bit_of(axis, distance=1):
    return (lax.axis_index(axis) // distance) % 2 == 1


def after(value, *others):
    return lax.optimization_barrier((value, *others))[0]


def fixed(value):
    return lax.optimization_barrier(value.astype(BF))


def gather_z(piece):
    lead = 0
    for distance in distances("z"):
        piece = join(piece, swap(piece, "z", distance), bit_of("z", distance), lead)
        lead += 1
    return piece.reshape(lax.axis_size("z"), *piece.shape[lead:])


def gather_yx(shard):
    piece = gather_z(shard)
    mine = join(piece, swap(piece, "y"), bit_of("y"), 1).reshape(-1, shard.shape[1])
    return mine, swap(mine, "x")


def gather_xy(shard):
    piece = gather_z(shard)
    other = swap(piece, "x")
    bit = bit_of("y")
    both = (join(p, swap(p, "y"), bit, 1) for p in (piece, other))
    return tuple(p.reshape(-1, shard.shape[1]) for p in both)


def take(value, bit, dim):
    low, high = (lax.index_in_dim(value, k, dim, keepdims=False) for k in (0, 1))
    keep = jnp.where(bit, high, low)
    send = jnp.where(bit, low, high)
    return keep, send


def halve(value, axis, bit, dim, distance=1, *wait):
    keep, send = take(value, bit, dim)
    got = swap(fixed(send), axis, distance)
    if wait:
        got = after(got, *wait)
    return keep.astype(F32) + got.astype(F32)


def scatter_z(value):
    steps = distances("z")
    value = value.reshape(*(2 for _ in steps), *value.shape[1:])
    for k in range(len(steps) - 1, -1, -1):
        value = halve(value, "z", bit_of("z", steps[k]), k, steps[k])
    return value


def by_rows(grad):
    return grad.reshape(lax.axis_size("z"), 2, -1, grad.shape[-1])


def all_sum(value, axes):
    for axis in axes:
        for distance in distances(axis):
            value = value + swap(value, axis, distance)
    return value


def swap_cores(own):
    half = own.shape[0] // 2
    return jnp.concatenate((swap(own[:half], "c"), swap(own[half:], "c")), axis=0)


def across_cores(partial_value):
    own = fixed(partial_value)
    return own.astype(F32) + swap_cores(own).astype(F32)


def both_bins(own):
    half = SLOTS // 2
    core = lax.axis_index("c")
    sent = lax.dynamic_slice_in_dim(own, core * half, half, axis=0)
    got = swap(sent, "x")
    other = join(got, swap(got, "c"), bit_of("c"), 0).reshape(own.shape)
    return join(own, other, bit_of("x"), 0).reshape(-1, D).astype(F32)


def layer_norm(rows, gain, shift):
    centre = rows - jnp.mean(rows, axis=-1, keepdims=True)
    spread = jnp.mean(centre * centre, axis=-1, keepdims=True)
    return centre * lax.rsqrt(spread + EPS) * gain + shift


def segments_of(seq_lengths, seq_bin, index):
    count = seq_lengths.shape[0]
    order = jnp.arange(count, dtype=jnp.int32)
    inside = seq_bin == index
    leader = jnp.min(jnp.where(inside, order, count))
    first = jnp.sum(jnp.where(order == leader, seq_lengths, 0))
    total = jnp.sum(jnp.where(inside, seq_lengths, 0))
    slot = jnp.arange(SLOTS, dtype=jnp.int32)
    segment = jnp.where(slot < first, 0, jnp.where(slot < total, 1, slot + 2))
    return (segment, slot < total)


def first_key(seq_lengths, seq_bin, index):
    segment, valid = segments_of(seq_lengths, seq_bin, index)
    slot = jnp.arange(SLOTS, dtype=jnp.int32)
    start = jnp.sum(jnp.where(segment == 0, 1, 0))
    low = jnp.where(segment == 0, 0, jnp.where(segment == 1, start, slot))
    return low, valid


def dot_nt(left, right):
    return lax.dot_general(left, right, (((1,), (1,)), ((), ())), preferred_element_type=F32)


def dot_tn(left, right):
    return lax.dot_general(left, right, (((0,), (0,)), ((), ())), preferred_element_type=F32)


def tile_mask(low, tile, keys):
    shape = (TILE, keys)
    row = lax.broadcasted_iota(jnp.int32, shape, 0) + tile * TILE
    column = lax.broadcasted_iota(jnp.int32, shape, 1)
    return (column <= row) & (column >= low)


def attend_kernel(low_ref, qkv_ref, out_ref, log_ref):
    width = out_ref.shape[1]
    for tile in range(SLOTS // TILE):
        here = slice(tile * TILE, (tile + 1) * TILE)
        keys = (tile + 1) * TILE
        mask = tile_mask(low_ref[here], tile, keys)
        for head in range(width // HEAD_DIM):
            lanes = slice(head * HEAD_DIM, (head + 1) * HEAD_DIM)
            query = qkv_ref[here, lanes]
            key = qkv_ref[:keys, width + head * HEAD_DIM : width + (head + 1) * HEAD_DIM]
            value = qkv_ref[:keys, 2 * width + head * HEAD_DIM : 2 * width + (head + 1) * HEAD_DIM]
            scores = jnp.where(mask, dot_nt(query, key), FLOOR)
            top = jnp.max(scores, axis=-1, keepdims=True)
            raised = jnp.exp(scores - top)
            total = jnp.sum(raised, axis=-1, keepdims=True)
            weights = (raised * (1.0 / total)).astype(BF)
            mixed = jnp.dot(weights, value, preferred_element_type=F32)
            out_ref[here, lanes] = mixed.astype(BF)
            log_ref[here, lanes] = jnp.broadcast_to(top + jnp.log(total), (TILE, HEAD_DIM))


def attend_back_kernel(low_ref, qkv_ref, grad_ref, log_ref, out_ref, keys_sum, values_sum):
    width = grad_ref.shape[1]
    for head in range(width // HEAD_DIM):
        lanes = slice(head * HEAD_DIM, (head + 1) * HEAD_DIM)
        key_lanes = slice(width + head * HEAD_DIM, width + (head + 1) * HEAD_DIM)
        value_lanes = slice(2 * width + head * HEAD_DIM, 2 * width + (head + 1) * HEAD_DIM)
        keys_sum[...] = jnp.zeros_like(keys_sum)
        values_sum[...] = jnp.zeros_like(values_sum)
        for tile in range(SLOTS // TILE):
            here = slice(tile * TILE, (tile + 1) * TILE)
            keys = (tile + 1) * TILE
            mask = tile_mask(low_ref[here], tile, keys)
            query = qkv_ref[here, lanes]
            key = qkv_ref[:keys, key_lanes]
            value = qkv_ref[:keys, value_lanes]
            grad = grad_ref[here, lanes]
            scores = dot_nt(query, key) - log_ref[here, head * HEAD_DIM : head * HEAD_DIM + 1]
            weights = jnp.exp(jnp.where(mask, scores, FLOOR))
            grad_weights = dot_nt(grad, value)
            product = weights * grad_weights
            inner = jnp.sum(product, axis=-1, keepdims=True)
            grad_scores = (product - weights * inner).astype(BF)
            values_sum[:keys] += dot_tn(weights.astype(BF), grad)
            keys_sum[:keys] += dot_tn(grad_scores, query)
            grad_query = jnp.dot(grad_scores, key, preferred_element_type=F32).astype(BF)
            out_ref[here, lanes] = (grad_query.astype(F32) * HEAD_DIM ** (-0.5)).astype(BF)
        out_ref[:, key_lanes] = keys_sum[...].astype(BF)
        out_ref[:, value_lanes] = values_sum[...].astype(BF)


def on_chip(kernel, shapes, scratch, flops, exps, *operands):
    moved = sum(o.size * o.dtype.itemsize for o in (*operands, *shapes))
    return pl.pallas_call(
        kernel,
        out_shape=shapes,
        in_specs=[pl.BlockSpec(memory_space=pltpu.VMEM)] * len(operands),
        out_specs=[pl.BlockSpec(memory_space=pltpu.VMEM)] * len(shapes),
        scratch_shapes=scratch,
        compiler_params=pltpu.CompilerParams(vmem_limit_bytes=50 * 2**20),
        cost_estimate=pl.CostEstimate(flops=flops, bytes_accessed=moved, transcendentals=exps),
    )(*operands)


def attend(low, qkv):
    width = qkv.shape[1] // 3
    shapes = [
        jax.ShapeDtypeStruct((SLOTS, width), BF),
        jax.ShapeDtypeStruct((SLOTS, width), F32),
    ]
    pairs = SLOTS * SLOTS * width // HEAD_DIM
    return on_chip(attend_kernel, shapes, [], 16 * pairs * HEAD_DIM, pairs, low, qkv)


def attend_back(low, qkv, grad, log_total):
    shapes = [jax.ShapeDtypeStruct(qkv.shape, BF)]
    scratch = [pltpu.VMEM((SLOTS, HEAD_DIM), F32)] * 2
    pairs = SLOTS * SLOTS * grad.shape[1] // HEAD_DIM
    return on_chip(
        attend_back_kernel, shapes, scratch, 40 * pairs * HEAD_DIM, pairs, low, qkv, grad, log_total
    )[0]


def newton_kernel(gram_ref, panel_ref, out_ref, ah, al, ph, pl_, bh, bl, qh, ql, rh, rl):
    def store(pair, here, value):
        high = value.astype(BF)
        pair[0][here] = high
        pair[1][here] = (value - high.astype(F32)).astype(BF)

    def product(left, right, here):
        total = jnp.dot(left[0][here], right[0][...], preferred_element_type=F32)
        total += jnp.dot(left[0][here], right[1][...], preferred_element_type=F32)
        return total + jnp.dot(left[1][here], right[0][...], preferred_element_type=F32)

    def tiles(body):
        @pl.loop(0, D // ROWS)
        def _(tile):
            first = pl.multiple_of(tile * ROWS, ROWS)
            body(first, pl.ds(first, ROWS))

    gram, poly, both = (ah, al), (ph, pl_), (bh, bl)
    total, spare = (qh, ql), (rh, rl)
    tiles(lambda first, here: store(gram, here, gram_ref[here]))
    for step in range(NS_STEPS):

        def make_poly(first, here):
            square = product(gram, gram, here)
            here_gram = gram[0][here].astype(F32) + gram[1][here].astype(F32)
            row = lax.broadcasted_iota(jnp.int32, (ROWS, D), 0) + first
            column = lax.broadcasted_iota(jnp.int32, (ROWS, D), 1)
            value = NS_B * here_gram + NS_C * square
            value = jnp.where(row == column, value + NS_A, value)
            store(poly, here, value)
            if step == 0:
                store(total, here, value)

        tiles(make_poly)
        if step > 0:
            tiles(lambda first, here: store(spare, here, product(poly, total, here)))
            total, spare = spare, total
        if step < NS_STEPS - 1:
            tiles(lambda first, here: store(both, here, product(poly, gram, here)))
            tiles(lambda first, here: store(gram, here, product(both, poly, here)))

    def finish(first, here):
        value = jnp.dot(total[0][here], panel_ref[...], preferred_element_type=F32)
        value += jnp.dot(total[1][here], panel_ref[...], preferred_element_type=F32)
        out_ref[here] = value

    tiles(finish)


def newton(gram, panel):
    factor = 1.0 / (jnp.sqrt(jnp.trace(gram)) + 1e-07)
    shapes = [jax.ShapeDtypeStruct(panel.shape, F32)]
    scratch = [pltpu.VMEM((D, D), BF)] * 10
    flops = 53 * 2 * D**3
    orth = on_chip(newton_kernel, shapes, scratch, flops, 0, gram * (factor * factor), panel)[0]
    return orth * factor


def gram_sum(gram):
    keep, send = take(gram.reshape(2, D // 2, D), bit_of("c"), 0)
    mine = keep + swap(send, "c")
    mine = mine + swap(mine, "x")
    return join(mine, swap(mine, "c"), bit_of("c"), 0).reshape(D, D)


def on_device(
    tokens,
    cotangent,
    seq_lengths,
    seq_bin,
    qkv_weight,
    out_weight,
    up_weight,
    down_weight,
    norm_gains,
    shared_biases,
    head_biases,
    unit_bias,
    qkv_moment,
    out_moment,
    up_moment,
    down_moment,
    gain_moment,
    bias_moment,
    head_moment,
    unit_moment,
):
    x_index = lax.axis_index("x")
    groups = lax.axis_size("z") * lax.axis_size("y")
    position = lax.axis_index("z") * lax.axis_size("y") + lax.axis_index("y")
    rows_each = qkv_weight.shape[1]
    heads_each = qkv_weight.shape[2]
    units_each = up_weight.shape[1]
    scale = HEAD_DIM ** (-0.5)

    qkv_shard = jnp.concatenate([qkv_weight[t] for t in range(3)], axis=1)
    qkv_own, qkv_next_x = gather_yx(qkv_shard)
    up_own, up_next_x = gather_yx(jnp.concatenate((up_weight, out_weight.T), axis=1))
    down = gather_xy(down_weight.T)
    qkv = (qkv_own, qkv_next_x)
    up = (up_own[:, :units_each], up_next_x[:, :units_each])
    out = (up_own[:, units_each:], up_next_x[:, units_each:])

    small = jnp.concatenate((head_biases.reshape(-1), unit_bias))
    small = (small, swap(small, "x"))
    zero = jnp.zeros((heads_each,), F32)
    scales = jnp.concatenate((jnp.full((heads_each,), scale, F32), jnp.ones((2 * heads_each,), F32)))

    def project(group):
        shift = jnp.concatenate(
            (small[group][:heads_each], zero, small[group][heads_each : 2 * heads_each])
        )
        value = jnp.dot(normed, qkv[group], preferred_element_type=F32)
        return ((value + shift) * scales).astype(BF)

    start = x_index * SLOTS
    rows = lax.dynamic_slice_in_dim(tokens, start, SLOTS, axis=0)
    low, valid = first_key(seq_lengths, seq_bin, position * 2 + x_index)
    low = low[:, None]
    source = rows.astype(F32)
    normed = layer_norm(source, norm_gains[0], shared_biases[0]).astype(BF)
    heads = [project(0)]
    mixed, logs = zip(attend(low, heads[0]))
    heads.append(after(project(1), mixed[0]))
    mixed_x, logs_x = attend(low, heads[1])
    mixed, logs = (mixed[0], mixed_x), (logs[0], logs_x)
    branch = across_cores(dot_nt(mixed[0], out[0]) + dot_nt(mixed[1], out[1]))
    hidden = source + (branch + shared_biases[2])
    normed_two = layer_norm(hidden, norm_gains[1], shared_biases[1]).astype(BF)
    before = [
        jnp.dot(normed_two, up[k], preferred_element_type=F32) + small[k][2 * heads_each :]
        for k in range(2)
    ]
    active = [jax.nn.gelu(b).astype(BF) for b in before]

    grad_rows = lax.dynamic_slice_in_dim(cotangent, start, SLOTS, axis=0)
    grad_rows = grad_rows * valid[:, None].astype(BF)
    grad_result = grad_rows.astype(F32)
    grad_before = [
        jax.vjp(jax.nn.gelu, before[k])[1](
            jnp.dot(grad_rows, down[k], preferred_element_type=F32)
        )[0].astype(BF)
        for k in range(2)
    ]
    grad_partial = fixed(dot_nt(grad_before[0], up[0]) + dot_nt(grad_before[1], up[1]))
    grad_other = swap_cores(grad_partial)
    planes = lax.axis_size("z")
    held, held_two = after(tuple(active), grad_partial), after(normed_two, grad_partial)
    grad_up = [dot_tn(held_two, grad_before[k]).astype(BF) for k in range(2)]
    grad_down = jnp.stack([by_rows(dot_tn(grad_rows, held[k]).astype(BF)) for k in range(2)])
    partial_two = fixed(dot_nt(active[0], down[0]) + dot_nt(active[1], down[1]))

    grad_normed_two = grad_partial.astype(F32) + grad_other.astype(F32)
    grad_hidden, grad_gain_two, grad_shift_two = jax.vjp(
        layer_norm, hidden, norm_gains[1], shared_biases[1]
    )[1](grad_normed_two)
    grad_hidden = grad_hidden + grad_result
    grad_branch = grad_hidden.astype(BF)
    grad_mixed = [jnp.dot(grad_branch, out[k], preferred_element_type=F32).astype(BF) for k in range(2)]
    back_x = attend_back(low, heads[1], grad_mixed[1], logs[1])
    grad_square_x = jnp.concatenate(
        (dot_tn(normed, back_x).astype(BF), dot_tn(grad_branch, mixed[1]).astype(BF)), axis=1
    )
    up_sum = grad_up[0].astype(F32) + after(swap(grad_up[1], "x"), back_x).astype(F32)
    down_sum = halve(grad_down, "y", bit_of("y"), 2, 1, back_x)
    square_got = swap(fixed(grad_square_x), "x")
    back = attend_back(low, heads[0], after(grad_mixed[0], back_x), logs[0])
    grad_square = jnp.concatenate(
        (dot_tn(normed, back).astype(BF), dot_tn(grad_branch, mixed[0]).astype(BF)), axis=1
    )
    up_sum = halve(by_rows(up_sum), "y", bit_of("y"), 1, 1, back)
    down_got = after(swap(fixed(down_sum[1]), "x"), back)
    down_sum = down_sum[0] + down_got.astype(F32)
    sum_up = scatter_z(up_sum)
    sum_down = scatter_z(down_sum)
    square = grad_square.astype(F32) + square_got.astype(F32)
    square = halve(by_rows(square), "y", bit_of("y"), 1)
    sum_square = scatter_z(square)

    grad_partial = fixed(dot_nt(back, qkv[0]) + dot_nt(back_x, qkv[1]))
    grad_normed = grad_partial.astype(F32) + swap_cores(grad_partial).astype(F32)
    grad_source, grad_gain_one, grad_shift_one = jax.vjp(
        layer_norm, source, norm_gains[0], shared_biases[0]
    )[1](grad_normed)
    result = hidden + (
        (partial_two.astype(F32) + swap_cores(partial_two).astype(F32)) + shared_biases[3]
    )
    block_out = both_bins(after(fixed(result), square))
    input_grad = both_bins(fixed(grad_hidden + grad_source))

    def by_x(mine, theirs):
        return join(mine, theirs, bit_of("x"), 1)

    grad_bias = [jnp.sum(b.astype(F32), axis=0) for b in (back, back_x)]
    grad_heads = [jnp.stack((g[:heads_each], g[2 * heads_each :])) for g in grad_bias]
    grad_units = [jnp.sum(g.astype(F32), axis=0)[None] for g in grad_before]
    vectors = (
        jnp.stack((grad_gain_one, grad_gain_two)),
        jnp.stack(
            (
                grad_shift_one,
                grad_shift_two,
                jnp.sum(grad_branch.astype(F32), axis=0),
                jnp.sum(grad_result, axis=0),
            )
        ),
        by_x(*grad_heads),
        by_x(*grad_units),
    )
    sizes = [v.size for v in vectors]
    flat = all_sum(
        jnp.concatenate([v.reshape(-1) for v in vectors]).reshape(-1, 128), ("x", "y", "z")
    ).reshape(-1)
    ends = [sum(sizes[: k + 1]) for k in range(4)]
    pieces = [flat[end - size : end] for end, size in zip(ends, sizes)]
    gains_sum = pieces[0].reshape(2, D)
    biases_sum = pieces[1].reshape(4, D)
    heads_sum = lax.dynamic_index_in_dim(
        pieces[2].reshape(2, 2, heads_each), x_index, 1, keepdims=False
    )
    units_sum = lax.dynamic_index_in_dim(pieces[3].reshape(2, units_each), x_index, 0, False)

    grads = (
        sum_square[:, :heads_each],
        sum_square[:, heads_each : 2 * heads_each],
        sum_square[:, 2 * heads_each : 3 * heads_each],
        sum_square[:, 3 * heads_each :],
        sum_up,
        sum_down,
    )
    moments = (
        qkv_moment[0],
        qkv_moment[1],
        qkv_moment[2],
        out_moment.T,
        up_moment,
        down_moment.T,
    )
    next_moments = [MOMENTUM * moment + grad for moment, grad in zip(moments, grads)]
    local_panels = [
        (grad + MOMENTUM * moment).astype(BF) for moment, grad in zip(next_moments, grads)
    ]
    spread = groups // 8
    owners = [number * spread for number in (0, 3, 4, 7, 2, 5)]

    def to_owners(width, numbers):
        outgoing = jnp.zeros((groups, rows_each, width), BF)
        for number in numbers:
            outgoing = outgoing.at[owners[number]].set(local_panels[number])
        incoming = lax.all_to_all(outgoing, ("z", "y"), split_axis=0, concat_axis=0, tiled=True)
        return incoming.reshape(groups * rows_each, width)

    wide = to_owners(units_each, (4, 5))
    wide_gram = gram_sum(dot_nt(wide, wide))
    narrow = to_owners(heads_each, (0, 1, 2, 3))
    narrow_x = swap(narrow, "x")
    pair = jnp.concatenate((narrow, narrow_x), axis=1)
    pair = jnp.concatenate((pair, swap(pair, "c")), axis=1)
    is_wide = (position == owners[4]) | (position == owners[5])
    gram = jnp.where(is_wide, wide_gram, dot_nt(pair, pair))
    narrow = jnp.pad(narrow, ((0, 0), (0, units_each - heads_each)))
    orth = newton(gram, jnp.where(is_wide, wide, narrow))
    back = lax.all_to_all(
        orth.astype(BF).reshape(groups, rows_each, units_each),
        ("z", "y"),
        split_axis=0,
        concat_axis=0,
        tiled=True,
    ).astype(F32)
    returned = [back[owners[k]][:, : local_panels[k].shape[1]] for k in range(6)]
    keep_share = 1.0 - RATE * DECAY
    up_factor = math.sqrt(max(1.0, FF / D))
    qkv_next = qkv_weight.astype(F32) * keep_share - RATE * jnp.stack(returned[:3])
    out_next = out_weight.astype(F32) * keep_share - RATE * returned[3].T
    up_next = up_weight.astype(F32) * keep_share - RATE * up_factor * returned[4]
    down_next = down_weight.astype(F32) * keep_share - RATE * returned[5].T
    rate_vector = VECTOR_RATE / math.sqrt(groups * tokens.shape[0])
    gain_moment_next = MOMENTUM * gain_moment + gains_sum
    bias_moment_next = MOMENTUM * bias_moment + biases_sum
    head_moment_next = MOMENTUM * head_moment + heads_sum
    unit_moment_next = MOMENTUM * unit_moment + units_sum
    gain_next = norm_gains - rate_vector * gain_moment_next
    bias_next = shared_biases - rate_vector * bias_moment_next
    head_next = head_biases - rate_vector * head_moment_next
    unit_next = unit_bias - rate_vector * unit_moment_next
    return (
        block_out,
        input_grad,
        jnp.stack(next_moments[:3]),
        qkv_next,
        next_moments[3].T,
        out_next,
        next_moments[4],
        up_next,
        next_moments[5].T,
        down_next,
        gain_moment_next,
        gain_next,
        bias_moment_next,
        bias_next,
        head_moment_next,
        head_next,
        unit_moment_next,
        unit_next,
    )


def solution(mesh):
    dp_size, mp_size = mesh.devices.shape
    split = Mesh(
        mesh.devices.reshape(dp_size // 2, 2, mp_size // 2, 2), ("z", "y", "x", "c")
    )
    dp, mp = ("z", "y"), ("x", "c")
    in_specs = (
        P(dp, None),
        P(dp, None),
        P(),
        P(),
        P(None, dp, mp),
        P(mp, dp),
        P(dp, mp),
        P(mp, dp),
        P(),
        P(),
        P(None, mp),
        P(mp),
        P(None, dp, mp),
        P(mp, dp),
        P(dp, mp),
        P(mp, dp),
        P(),
        P(),
        P(None, mp),
        P(mp),
    )
    out_specs = (
        P(dp, None),
        P(dp, None),
        P(None, dp, mp),
        P(None, dp, mp),
        P(mp, dp),
        P(mp, dp),
        P(dp, mp),
        P(dp, mp),
        P(mp, dp),
        P(mp, dp),
        P(),
        P(),
        P(),
        P(),
        P(None, mp),
        P(None, mp),
        P(mp),
        P(mp),
    )
    return jax.shard_map(
        on_device, mesh=split, in_specs=in_specs, out_specs=out_specs, check_vma=False
    )
```

time: 733 us -> 519 us (0.71)
  matrix products: 229 us -> 60.4 us
  Pallas kernels: 0 us -> 97.1 us
  blocking collectives: 74.3 us -> 0 us
  local copies, waits for them, and re-layouts: 69.6 us -> 27.8 us
  other arithmetic: 112 us -> 90.9 us
  starting transfers between devices: 72.9 us -> 65.4 us
    dot_general x36 -> x26, matrix products: 228 us -> 60.4 us  [the longest x10 22.8 us: dot_nt(): lax.dot_general(left, right, (((1,), (1,)), ((), ())), preferred_element_...]
    pallas_call x0 -> x5, Pallas kernels: none -> 97.1 us  [on_chip(): pl.pallas_call(kernel, out_shape=shapes, in_specs=[pl.BlockSpec(memory_sp...]
    psum x1 -> x0, blocking collectives: 74.3 us -> none  [on_device(): lax.psum(jnp.concatenate([v.reshape(-1) for v in vectors]), ('z', 'y', 'x'))]
    another operation x9 -> x0, local copies, waits for them, and re-layouts: 17.9 us -> none  [the longest x2 14.5 us: on_device(): weights_qkv = qkv_full.reshape(2, D, 3, heads_each)]
    ppermute x60 -> x47, waiting for transfers between devices: 132 us -> 148 us  [swap(): return lax.ppermute(value, axis, [(i, i ^ distance) for i in range(size)])]
    convert_element_type x19 -> x3, other arithmetic: 19.8 us -> 3.26 us  [the longest x1 1.47 us: on_device(): back = lax.all_to_all(orth.astype(BF).reshape(groups, rows_each, units_ea...]
    all_to_all x2 -> x3, waiting for transfers between devices: 33.3 us -> 19.1 us  [the longest x1 19 us: on_device(): lax.all_to_all(orth.astype(BF).reshape(groups, rows_each, units_each), ('...]
    ppermute x60 -> x47, starting transfers between devices: 62.7 us -> 50.1 us  [swap(): return lax.ppermute(value, axis, [(i, i ^ distance) for i in range(size)])]
  transfers between devices with their start and end apart: 62 -> 50, of which waited for: 30 -> 20; matrix products, arithmetic and copies ran while one was open for 38% -> 27% of each run, Pallas kernels for 0% -> 19%
where the time goes in v2:
time: 519 us; the launch traced here: 513 us
  waiting for transfers between devices  167 us (32%)
  Pallas kernels  97.1 us (19%)
  other arithmetic  90.9 us (18%)
  starting transfers between devices  65.4 us (13%)
  matrix products  60.4 us (12%)
  local copies, waits for them, and re-layouts  27.8 us (5%)
    ppermute x47, waiting for transfers between devices, swap(): return lax.ppermute(value, axis, [(i, i ^ distance) for i in range(size)])  148 us
    pallas_call x5, Pallas kernels, on_chip(): pl.pallas_call(kernel, out_shape=shapes, in_specs=[pl.BlockSpec(memory_sp...  97.1 us
    ppermute x47, starting transfers between devices, swap(): return lax.ppermute(value, axis, [(i, i ^ distance) for i in range(size)])  50.1 us
    dot_general x10, matrix products, dot_nt(): lax.dot_general(left, right, (((1,), (1,)), ((), ())), preferred_element_...  22.8 us
    all_to_all x1, waiting for transfers between devices, on_device(): lax.all_to_all(orth.astype(BF).reshape(groups, rows_each, units_each), ('...  19 us
    dot_general x8, matrix products, dot_tn(): lax.dot_general(left, right, (((0,), (0,)), ((), ())), preferred_element_...  13.9 us
    another operation x30, other arithmetic, join(): return jnp.stack((low, high), axis=dim)  12.7 us
    reduce_sum x4, other arithmetic, layer_norm(): centre = rows - jnp.mean(rows, axis=-1, keepdims=True)  11.8 us
  transfers between devices with their start and end apart: 50, of which 20 were waited for; matrix products, arithmetic and copies ran while one was open for 27% of the time, Pallas kernels for 19%

profile of v2, /device:TPU:0, one launch (start us, length us, event | category | flops | bytes accessed | tf_op | source)
XLA Modules:
  0.0 512.6 jit_solution(16005845127626101144)
XLA Ops:
  2.1 3.0 collective-permute-start.7
  11.0 2.7 collective-permute-start.3
  31.7 3.4 collective-permute-done.1
  36.8 6.7 %collective-permute-done.4 = bf16[2,96,960]{2,1,0:T(8,128)(2,1)S(1)} collective-permute-done((bf16[2,96,960]{2,1,0:T(8,128)(2,1)S(1)}, bf16[2,96,960]{2,1,0:T(8,128)(2,1)S(1)}, u32[]{:S(2)}, u32[]{:S(2)}) %collective-permute-start.4) | collective-permute-done | bytes 368672 | tf_op jit(solution)/shard_map/ppermute | solution.py:34
  45.2 4.0 collective-permute-done.12
  55.4 10.9 %collective-permute-done.5 = bf16[4,96,960]{2,1,0:T(8,128)(2,1)S(1)} collective-permute-done((bf16[4,96,960]{2,1,0:T(8,128)(2,1)S(1)}, bf16[4,96,960]{2,1,0:T(8,128)(2,1)S(1)}, u32[]{:S(2)}, u32[]{:S(2)}) %collective-permute-start.5) | collective-permute-done | bytes 737312 | tf_op jit(solution)/shard_map/ppermute | solution.py:34
  69.2 3.0 multiply_convert_fusion.3.qkv_ref
  72.2 6.2 %shard_map.331 = (bf16[1024,192]{1,0:T(8,128)(2,1)S(1)}, f32[1024,192]{1,0:T(8,128)S(1)}) custom-call(s32[1024,1]{1,0:T(8,128)S(1)} %select_select_fusion.low_ref, bf16[1024,576]{1,0:T(8,128)(2,1)S(1)} %multiply_convert_fusion.3.qkv_ref), custom_call_target="tpu_custom_call" | custom-call | flops 3221225472 | bytes 2363392 | tf_op jit(solution)/shard_map/pallas_call | solution.py:233
  80.7 5.0 collective-permute-done.6
  85.7 2.8 multiply_convert_fusion.2.qkv_ref
  88.5 6.6 %shard_map.332 = (bf16[1024,192]{1,0:T(8,128)(2,1)S(1)}, f32[1024,192]{1,0:T(8,128)S(1)}) custom-call(s32[1024,1]{1,0:T(8,128)S(1)} %select_select_fusion.low_ref, bf16[1024,576]{1,0:T(8,128)(2,1)S(1)} %multiply_convert_fusion.2.qkv_ref), custom_call_target="tpu_custom_call" | custom-call | flops 3221225472 | bytes 2363392 | tf_op jit(solution)/shard_map/pallas_call | solution.py:233
  95.1 20.7 %collective-permute-done.8 = bf16[768,960]{0,1:T(8,128)(2,1)} collective-permute-done((bf16[768,960]{0,1:T(8,128)(2,1)}, bf16[768,960]{0,1:T(8,128)(2,1)}, u32[]{:S(2)}, u32[]{:S(2)}) %collective-permute-start.8) | collective-permute-done | bytes 1474592 | tf_op jit(solution)/shard_map/ppermute | solution.py:34
  123.9 3.1 multiply_convert_fusion.1
  127.0 3.5 convert_reduce_fusion.2
  131.9 4.3 multiply_convert_fusion
  136.3 3.6 convert_reduce_fusion.3
  139.9 3.2 add_convert_fusion.2
  144.5 3.3 fusion.114
  163.3 3.0 multiply_reduce_fusion
  166.4 4.6 fusion.103
  178.1 10.5 %shard_map.333 = bf16[1024,576]{1,0:T(8,128)(2,1)S(1)} custom-call(s32[1024,1]{1,0:T(8,128)S(1)} %select_select_fusion.low_ref, bf16[1024,576]{1,0:T(8,128)(2,1)} %copy-done, bf16[1024,192]{1,0:T(8,128)(2,1)S(1)} %copy.136.grad_ref, f32[1024,192]{1,0:T(8,128)S(1)} %copy-done.5), custom_call_target="tpu_custom_call" | custom-call | flops 8053063680 | bytes 3543040 | tf_op jit(solution)/shard_map/pallas_call | solution.py:233
  188.9 10.7 %shard_map.334 = bf16[1024,576]{1,0:T(8,128)(2,1)S(1)} custom-call(s32[1024,1]{1,0:T(8,128)S(1)} %select_select_fusion.low_ref, bf16[1024,576]{1,0:T(8,128)(2,1)} %copy-done.1, bf16[1024,192]{1,0:T(8,128)(2,1)S(1)} %convolution_convert_fusion.6.grad_ref, f32[1024,192]{1,0:T(8,128)S(1)} %copy-done.3), custom_call_target="tpu_custom_call" | custom-call | flops 8053063680 | bytes 3543040 | tf_op jit(solution)/shard_map/pallas_call | solution.py:233
  205.6 3.7 add_convert_fusion.1
  229.1 4.7 fusion.102
  233.9 17.8 %collective-permute-done.43 = f32[54,128]{1,0:T(8,128)S(1)} collective-permute-done((f32[54,128]{1,0:T(8,128)S(1)}, f32[54,128]{1,0:T(8,128)S(1)}, u32[]{:S(2)}, u32[]{:S(2)}) %collective-permute-start.43) | collective-permute-done | bytes 27680 | tf_op jit(solution)/shard_map/ppermute | solution.py:34
  252.8 2.8 collective-permute-done.44
  263.1 8.1 %collective-permute-done.32 = bf16[2,96,768]{2,1,0:T(8,128)(2,1)S(1)} collective-permute-done((bf16[2,96,768]{2,1,0:T(8,128)(2,1)S(1)}, bf16[2,96,768]{2,1,0:T(8,128)(2,1)S(1)}, u32[]{:S(2)}, u32[]{:S(2)}) %collective-permute-start.32) | collective-permute-done | bytes 294944 | tf_op jit(solution)/shard_map/ppermute | solution.py:34
  271.4 3.4 collective-permute-done.36
  275.2 5.4 %collective-permute-done.33 = bf16[96,768]{1,0:T(8,128)(2,1)S(1)} collective-permute-done((bf16[96,768]{1,0:T(8,128)(2,1)S(1)}, bf16[96,768]{1,0:T(8,128)(2,1)S(1)}, u32[]{:S(2)}, u32[]{:S(2)}) %collective-permute-start.33) | collective-permute-done | bytes 147488 | tf_op jit(solution)/shard_map/ppermute | solution.py:34
  285.1 4.9 all-to-all-start
  290.1 2.8 add_convert_fusion
  295.9 12.7 %collective-permute-done.46 = f32[54,128]{1,0:T(8,128)S(1)} collective-permute-done((f32[54,128]{1,0:T(8,128)S(1)}, f32[54,128]{1,0:T(8,128)S(1)}, u32[]{:S(2)}, u32[]{:S(2)}) %collective-permute-start.46) | collective-permute-done | bytes 27680 | tf_op jit(solution)/shard_map/ppermute | solution.py:34
  312.6 3.0 convert_add_fusion.6
  320.4 2.8 fusion.116
  323.5 8.3 %collective-permute-done.21 = bf16[4,96,768]{2,1,0:T(8,128)(2,1)} collective-permute-done((bf16[4,96,768]{2,1,0:T(8,128)(2,1)}, bf16[4,96,768]{2,1,0:T(8,128)(2,1)}, u32[]{:S(2)}, u32[]{:S(2)}) %collective-permute-start.21) | collective-permute-done | bytes 589856 | tf_op jit(solution)/shard_map/ppermute | solution.py:34
  337.6 2.9 collective-permute-done.28
  340.6 5.5 %collective-permute-start.29 = (bf16[96,768]{1,0:T(8,128)(2,1)S(1)}, bf16[96,768]{1,0:T(8,128)(2,1)S(1)}, u32[]{:S(2)}, u32[]{:S(2)}) collective-permute-start(bf16[96,768]{1,0:T(8,128)(2,1)S(1)} %fusion.68), channel_id=1, source_target_pairs={{0,16},{8,24},{16,0},{24,8},{1,17},{9,25},{17,1},{25,9},{2,18},{10... | collective-permute-start | bytes 442376 | tf_op jit(solution)/shard_map/ppermute | solution.py:34
  346.3 3.4 collective-permute-done.29
  354.1 4.7 all-to-all-start.1
  360.5 22.5 %collective-permute-done.39 = f32[384,768]{1,0:T(8,128)S(1)} collective-permute-done((f32[384,768]{1,0:T(8,128)S(1)}, f32[384,768]{1,0:T(8,128)S(1)}, u32[]{:S(2)}, u32[]{:S(2)}) %collective-permute-start.39) | collective-permute-done | bytes 1179680 | tf_op jit(solution)/shard_map/ppermute | solution.py:34
  389.8 7.6 %collective-permute-done.41 = bf16[768,192]{1,0:T(8,128)(2,1)S(1)} collective-permute-done((bf16[768,192]{1,0:T(8,128)(2,1)S(1)}, bf16[768,192]{1,0:T(8,128)(2,1)S(1)}, u32[]{:S(2)}, u32[]{:S(2)}) %collective-permute-start.41) | collective-permute-done | bytes 294944 | tf_op jit(solution)/shard_map/ppermute | solution.py:34
  401.2 3.3 select_reduce_fusion
  405.1 3.2 broadcast_multiply_fusion.gram_ref
  408.4 63.1 %shard_map.335 = f32[768,768]{1,0:T(8,128)S(1)} custom-call(f32[768,768]{1,0:T(8,128)} %broadcast_multiply_fusion.gram_ref, bf16[768,768]{1,0:T(8,128)(2,1)S(1)} %pad_select_fusion.panel_ref), custom_call_target="tpu_custom_call" | custom-call | flops 48016392192 | bytes 5898240 | tf_op jit(solution)/shard_map/pallas_call | solution.py:233
  472.7 5.7 %all-to-all-start.2 = ((bf16[8,96,768]{2,1,0:T(8,128)(2,1)}), bf16[8,96,768]{2,1,0:T(8,128)(2,1)}, u32[]{:S(2)}, u32[]{:S(2)}) async-start(bf16[8,96,768]{2,1,0:T(8,128)(2,1)} %bitcast.398), calls=%async_computation.2 | async-start | bytes 2359296 | tf_op jit(solution)/shard_map/all_to_all | solution.py:525
  478.4 3.4 bitcast_convert_fusion
  485.3 3.4 bitcast_convert_fusion.1
  488.7 19.0 %all-to-all-done.2 = bf16[8,96,768]{2,1,0:T(8,128)(2,1)} async-done(((bf16[8,96,768]{2,1,0:T(8,128)(2,1)}), bf16[8,96,768]{2,1,0:T(8,128)(2,1)}, u32[]{:S(2)}, u32[]{:S(2)}) %all-to-all-start.2) | async-done | bytes 1179680 | tf_op jit(solution)/shard_map/all_to_all | solution.py:525
  (457 shorter events, 156.4 us)
Async XLA Ops:
  2.1 23.6 %collective-permute-start.7 = (f32[1152]{0:T(1024)S(1)}, f32[1152]{0:T(1024)S(1)}, u32[]{:S(2)}, u32[]{:S(2)}) collective-permute-start(f32[1152]{0:T(1024)S(1)} %pad_maximum_fusion.24), channel_id=1, source_target_pairs={{0,2},{2,0},{1,3},{3,1},{4,6},{6,4},{5,7},{7,5},{8,10},{10,8},{9,1... | collective-permute-start | bytes 13832 | tf_op jit(solution)/shard_map/ppermute | solution.py:34
  6.1 19.8 %collective-permute-start = (bf16[96,576]{1,0:T(8,128)(2,1)S(1)}, bf16[96,576]{1,0:T(8,128)(2,1)S(1)}, u32[]{:S(2)}, u32[]{:S(2)}) collective-permute-start(bf16[96,576]{1,0:T(8,128)(2,1)S(1)} %pad_maximum_fusion.22), channel_id=1, source_target_pairs={{0,16},{8,24},{16,0},{24,8},{1,17},{9,25},{17,1},{25,9},{2,18},{10... | collective-permute-start | bytes 331784 | tf_op jit(solution)/shard_map/ppermute | solution.py:34
  8.8 19.0 %collective-permute-start.11 = (bf16[96,768]{1,0:T(8,128)(2,1)}, bf16[96,768]{1,0:T(8,128)(2,1)S(1)}, u32[]{:S(2)}, u32[]{:S(2)}) collective-permute-start(bf16[96,768]{1,0:T(8,128)(2,1)} %bitcast.418), channel_id=1, source_target_pairs={{0,16},{8,24},{16,0},{24,8},{1,17},{9,25},{17,1},{25,9},{2,18},{10... | collective-permute-start | bytes 442376 | tf_op jit(solution)/shard_map/ppermute | solution.py:34
  11.0 18.4 %collective-permute-start.3 = (bf16[96,960]{1,0:T(8,128)(2,1)S(1)}, bf16[96,960]{1,0:T(8,128)(2,1)S(1)}, u32[]{:S(2)}, u32[]{:S(2)}) collective-permute-start(bf16[96,960]{1,0:T(8,128)(2,1)S(1)} %pad_maximum_fusion.21), channel_id=1, source_target_pairs={{0,16},{8,24},{16,0},{24,8},{1,17},{9,25},{17,1},{25,9},{2,18},{10... | collective-permute-start | bytes 552968 | tf_op jit(solution)/shard_map/ppermute | solution.py:34
  26.1 9.0 %collective-permute-start.1 = (bf16[2,96,576]{2,1,0:T(8,128)(2,1)S(1)}, bf16[2,96,576]{2,1,0:T(8,128)(2,1)S(1)}, u32[]{:S(2)}, u32[]{:S(2)}) collective-permute-start(bf16[2,96,576]{2,1,0:T(8,128)(2,1)S(1)} %pad_maximum_fusion.20), channel_id=1, source_target_pairs={{0,8},{8,0},{16,24},{24,16},{1,9},{9,1},{17,25},{25,17},{2,10},{10... | collective-permute-start | bytes 663560 | tf_op jit(solution)/shard_map/ppermute | solution.py:34
  29.5 14.0 %collective-permute-start.4 = (bf16[2,96,960]{2,1,0:T(8,128)(2,1)S(1)}, bf16[2,96,960]{2,1,0:T(8,128)(2,1)S(1)}, u32[]{:S(2)}, u32[]{:S(2)}) collective-permute-start(bf16[2,96,960]{2,1,0:T(8,128)(2,1)S(1)} %pad_maximum_fusion.17), channel_id=1, source_target_pairs={{0,8},{8,0},{16,24},{24,16},{1,9},{9,1},{17,25},{25,17},{2,10},{10... | collective-permute-start | bytes 1105928 | tf_op jit(solution)/shard_map/ppermute | solution.py:34
  30.2 19.1 %collective-permute-start.12 = (bf16[2,96,768]{2,1,0:T(8,128)(2,1)S(1)}, bf16[2,96,768]{2,1,0:T(8,128)(2,1)S(1)}, u32[]{:S(2)}, u32[]{:S(2)}) collective-permute-start(bf16[2,96,768]{2,1,0:T(8,128)(2,1)S(1)} %pad_maximum_fusion.18), channel_id=1, source_target_pairs={{0,8},{8,0},{16,24},{24,16},{1,9},{9,1},{17,25},{25,17},{2,10},{10... | collective-permute-start | bytes 884744 | tf_op jit(solution)/shard_map/ppermute | solution.py:34
  35.2 17.0 %collective-permute-start.2 = (bf16[4,96,576]{2,1,0:T(8,128)(2,1)S(1)}, bf16[4,96,576]{2,1,0:T(8,128)(2,1)S(1)}, u32[]{:S(2)}, u32[]{:S(2)}) collective-permute-start(bf16[4,96,576]{2,1,0:T(8,128)(2,1)S(1)} %bitcast.411), channel_id=1, source_target_pairs={{0,4},{4,0},{1,5},{5,1},{2,6},{6,2},{3,7},{7,3},{8,12},{12,8},{9,1... | collective-permute-start | bytes 1327112 | tf_op jit(solution)/shard_map/ppermute | solution.py:34
  43.7 22.7 %collective-permute-start.5 = (bf16[4,96,960]{2,1,0:T(8,128)(2,1)S(1)}, bf16[4,96,960]{2,1,0:T(8,128)(2,1)S(1)}, u32[]{:S(2)}, u32[]{:S(2)}) collective-permute-start(bf16[4,96,960]{2,1,0:T(8,128)(2,1)S(1)} %bitcast.410), channel_id=1, source_target_pairs={{0,4},{4,0},{1,5},{5,1},{2,6},{6,2},{3,7},{7,3},{8,12},{12,8},{9,1... | collective-permute-start | bytes 2211848 | tf_op jit(solution)/shard_map/ppermute | solution.py:34
  50.2 28.2 %collective-permute-start.14 = (bf16[4,96,768]{2,1,0:T(8,128)(2,1)}, bf16[4,96,768]{2,1,0:T(8,128)(2,1)}, u32[]{:S(2)}, u32[]{:S(2)}) collective-permute-start(bf16[4,96,768]{2,1,0:T(8,128)(2,1)} %bitcast.30), channel_id=1, source_target_pairs={{0,2},{2,0},{1,3},{3,1},{4,6},{6,4},{5,7},{7,5},{8,10},{10,8},{9,1... | collective-permute-start | bytes 1769480 | tf_op jit(solution)/shard_map/ppermute | solution.py:34
  50.7 67.4 %collective-permute-start.13 = (bf16[4,96,768]{2,1,0:T(8,128)(2,1)}, bf16[4,96,768]{2,1,0:T(8,128)(2,1)}, u32[]{:S(2)}, u32[]{:S(2)}) collective-permute-start(bf16[4,96,768]{2,1,0:T(8,128)(2,1)} %bitcast.30), channel_id=1, source_target_pairs={{0,4},{4,0},{1,5},{5,1},{2,6},{6,2},{3,7},{7,3},{8,12},{12,8},{9,1... | collective-permute-start | bytes 1769480 | tf_op jit(solution)/shard_map/ppermute | solution.py:34
  53.9 31.8 %collective-permute-start.6 = (bf16[768,576]{0,1:T(8,128)(2,1)}, bf16[768,576]{0,1:T(8,128)(2,1)}, u32[]{:S(2)}, u32[]{:S(2)}) collective-permute-start(bf16[768,576]{0,1:T(8,128)(2,1)} %copy.129), channel_id=1, source_target_pairs={{0,2},{2,0},{1,3},{3,1},{4,6},{6,4},{5,7},{7,5},{8,10},{10,8},{9,1... | collective-permute-start | bytes 2654216 | tf_op jit(solution)/shard_map/ppermute | solution.py:34
  68.7 47.1 %collective-permute-start.8 = (bf16[768,960]{0,1:T(8,128)(2,1)}, bf16[768,960]{0,1:T(8,128)(2,1)}, u32[]{:S(2)}, u32[]{:S(2)}) collective-permute-start(bf16[768,960]{0,1:T(8,128)(2,1)} %copy.131), channel_id=1, source_target_pairs={{0,2},{2,0},{1,3},{3,1},{4,6},{6,4},{5,7},{7,5},{8,10},{10,8},{9,1... | collective-permute-start | bytes 4423688 | tf_op jit(solution)/shard_map/ppermute | solution.py:34
  78.4 41.2 %collective-permute-start.15 = (bf16[4,96,768]{2,1,0:T(8,128)(2,1)}, bf16[4,96,768]{2,1,0:T(8,128)(2,1)S(1)}, u32[]{:S(2)}, u32[]{:S(2)}) collective-permute-start(bf16[4,96,768]{2,1,0:T(8,128)(2,1)} %collective-permute-done.14), channel_id=1, source_target_pairs={{0,4},{4,0},{1,5},{5,1},{2,6},{6,2},{3,7},{7,3},{8,12},{12,8},{9,1... | collective-permute-start | bytes 1769480 | tf_op jit(solution)/shard_map/ppermute | solution.py:34
  117.5 3.9 collective-permute-start.9
  149.4 16.9 %collective-permute-start.16 = (bf16[512,768]{1,0:T(8,128)(2,1)S(1)}, bf16[512,768]{1,0:T(8,128)(2,1)S(1)}, u32[]{:S(2)}, u32[]{:S(2)}) collective-permute-start(bf16[512,768]{1,0:T(8,128)(2,1)S(1)} %get-tuple-element.242), channel_id=1, source_target_pairs={{0,1},{1,0},{2,3},{3,2},{4,5},{5,4},{6,7},{7,6},{8,9},{9,8},{10,11... | collective-permute-start | bytes 2359304 | tf_op jit(solution)/shard_map/ppermute | solution.py:34
  149.6 16.8 %collective-permute-start.17 = (bf16[512,768]{1,0:T(8,128)(2,1)S(1)}, bf16[512,768]{1,0:T(8,128)(2,1)S(1)}, u32[]{:S(2)}, u32[]{:S(2)}) collective-permute-start(bf16[512,768]{1,0:T(8,128)(2,1)S(1)} %get-tuple-element.243), channel_id=1, source_target_pairs={{0,1},{1,0},{2,3},{3,2},{4,5},{5,4},{6,7},{7,6},{8,9},{9,8},{10,11... | collective-permute-start | bytes 2359304 | tf_op jit(solution)/shard_map/ppermute | solution.py:34
  155.3 7.5 %collective-permute-start.18 = (bf16[512,768]{1,0:T(8,128)(2,1)S(1)}, bf16[512,768]{1,0:T(8,128)(2,1)S(1)}, u32[]{:S(2)}, u32[]{:S(2)}) collective-permute-start(bf16[512,768]{1,0:T(8,128)(2,1)S(1)} %copy-done.52), channel_id=1, source_target_pairs={{0,1},{1,0},{2,3},{3,2},{4,5},{5,4},{6,7},{7,6},{8,9},{9,8},{10,11... | collective-permute-start | bytes 2359304 | tf_op jit(solution)/shard_map/ppermute | solution.py:34
  155.4 7.9 %collective-permute-start.19 = (bf16[512,768]{1,0:T(8,128)(2,1)S(1)}, bf16[512,768]{1,0:T(8,128)(2,1)S(1)}, u32[]{:S(2)}, u32[]{:S(2)}) collective-permute-start(bf16[512,768]{1,0:T(8,128)(2,1)S(1)} %copy-done.51), channel_id=1, source_target_pairs={{0,1},{1,0},{2,3},{3,2},{4,5},{5,4},{6,7},{7,6},{8,9},{9,8},{10,11... | collective-permute-start | bytes 2359304 | tf_op jit(solution)/shard_map/ppermute | solution.py:34
  161.3 55.5 %collective-permute-start.34 = (bf16[2,4,96,768]{3,2,1,0:T(8,128)(2,1)}, bf16[2,4,96,768]{3,2,1,0:T(8,128)(2,1)}, u32[]{:S(2)}, u32[]{:S(2)}) collective-permute-start(bf16[2,4,96,768]{3,2,1,0:T(8,128)(2,1)} %select_bitcast_fusion.2), channel_id=1, source_target_pairs={{0,4},{4,0},{1,5},{5,1},{2,6},{6,2},{3,7},{7,3},{8,12},{12,8},{9,1... | collective-permute-start | bytes 3538952 | tf_op jit(solution)/shard_map/ppermute | solution.py:34
  162.8 54.0 %collective-permute-start.30 = (bf16[768,768]{1,0:T(8,128)(2,1)}, bf16[768,768]{1,0:T(8,128)(2,1)}, u32[]{:S(2)}, u32[]{:S(2)}) collective-permute-start(bf16[768,768]{1,0:T(8,128)(2,1)} %convolution_convert_fusion.2), channel_id=1, source_target_pairs={{0,2},{2,0},{1,3},{3,1},{4,6},{6,4},{5,7},{7,5},{8,10},{10,8},{9,1... | collective-permute-start | bytes 3538952 | tf_op jit(solution)/shard_map/ppermute | solution.py:34
  210.6 102.0 %collective-permute-start.20 = (bf16[768,768]{0,1:T(8,128)(2,1)}, bf16[768,768]{0,1:T(8,128)(2,1)}, u32[]{:S(2)}, u32[]{:S(2)}) collective-permute-start(bf16[768,768]{0,1:T(8,128)(2,1)} %pad_maximum_fusion.11), channel_id=1, source_target_pairs={{0,2},{2,0},{1,3},{3,1},{4,6},{6,4},{5,7},{7,5},{8,10},{10,8},{9,1... | collective-permute-start | bytes 3538952 | tf_op jit(solution)/shard_map/ppermute | solution.py:34
  212.5 12.3 %collective-permute-start.24 = (bf16[512,768]{1,0:T(8,128)(2,1)S(1)}, bf16[512,768]{1,0:T(8,128)(2,1)S(1)}, u32[]{:S(2)}, u32[]{:S(2)}) collective-permute-start(bf16[512,768]{1,0:T(8,128)(2,1)S(1)} %get-tuple-element.236), channel_id=1, source_target_pairs={{0,1},{1,0},{2,3},{3,2},{4,5},{5,4},{6,7},{7,6},{8,9},{9,8},{10,11... | collective-permute-start | bytes 2359304 | tf_op jit(solution)/shard_map/ppermute | solution.py:34
  212.5 12.3 %collective-permute-start.25 = (bf16[512,768]{1,0:T(8,128)(2,1)S(1)}, bf16[512,768]{1,0:T(8,128)(2,1)S(1)}, u32[]{:S(2)}, u32[]{:S(2)}) collective-permute-start(bf16[512,768]{1,0:T(8,128)(2,1)S(1)} %get-tuple-element.237), channel_id=1, source_target_pairs={{0,1},{1,0},{2,3},{3,2},{4,5},{5,4},{6,7},{7,6},{8,9},{9,8},{10,11... | collective-permute-start | bytes 2359304 | tf_op jit(solution)/shard_map/ppermute | solution.py:34
  223.6 34.2 %collective-permute-start.35 = (bf16[4,96,768]{2,1,0:T(8,128)(2,1)}, bf16[4,96,768]{2,1,0:T(8,128)(2,1)}, u32[]{:S(2)}, u32[]{:S(2)}) collective-permute-start(bf16[4,96,768]{2,1,0:T(8,128)(2,1)} %fusion.51), channel_id=1, source_target_pairs={{0,2},{2,0},{1,3},{3,1},{4,6},{6,4},{5,7},{7,5},{8,10},{10,8},{9,1... | collective-permute-start | bytes 1769480 | tf_op jit(solution)/shard_map/ppermute | solution.py:34
  224.3 33.5 %collective-permute-start.31 = (bf16[4,96,768]{2,1,0:T(8,128)(2,1)}, bf16[4,96,768]{2,1,0:T(8,128)(2,1)}, u32[]{:S(2)}, u32[]{:S(2)}) collective-permute-start(bf16[4,96,768]{2,1,0:T(8,128)(2,1)} %fusion.50), channel_id=1, source_target_pairs={{0,4},{4,0},{1,5},{5,1},{2,6},{6,2},{3,7},{7,3},{8,12},{12,8},{9,1... | collective-permute-start | bytes 1769480 | tf_op jit(solution)/shard_map/ppermute | solution.py:34
  227.7 24.0 %collective-permute-start.43 = (f32[54,128]{1,0:T(8,128)S(1)}, f32[54,128]{1,0:T(8,128)S(1)}, u32[]{:S(2)}, u32[]{:S(2)}) collective-permute-start(f32[54,128]{1,0:T(8,128)S(1)} %maximum_bitcast_fusion), channel_id=1, source_target_pairs={{0,2},{2,0},{1,3},{3,1},{4,6},{6,4},{5,7},{7,5},{8,10},{10,8},{9,1... | collective-permute-start | bytes 82952 | tf_op jit(solution)/shard_map/ppermute | solution.py:34
  251.7 3.9 collective-permute-start.44
  255.7 37.3 %collective-permute-start.45 = (f32[54,128]{1,0:T(8,128)S(1)}, f32[54,128]{1,0:T(8,128)S(1)}, u32[]{:S(2)}, u32[]{:S(2)}) collective-permute-start(f32[54,128]{1,0:T(8,128)S(1)} %fusion.152), channel_id=1, source_target_pairs={{0,16},{8,24},{16,0},{24,8},{1,17},{9,25},{17,1},{25,9},{2,18},{10... | collective-permute-start | bytes 82952 | tf_op jit(solution)/shard_map/ppermute | solution.py:34
  259.1 12.0 %collective-permute-start.32 = (bf16[2,96,768]{2,1,0:T(8,128)(2,1)S(1)}, bf16[2,96,768]{2,1,0:T(8,128)(2,1)S(1)}, u32[]{:S(2)}, u32[]{:S(2)}) collective-permute-start(bf16[2,96,768]{2,1,0:T(8,128)(2,1)S(1)} %fusion.60), channel_id=1, source_target_pairs={{0,8},{8,0},{16,24},{24,16},{1,9},{9,1},{17,25},{25,17},{2,10},{10... | collective-permute-start | bytes 884744 | tf_op jit(solution)/shard_map/ppermute | solution.py:34
  263.0 11.8 %collective-permute-start.36 = (bf16[2,96,768]{2,1,0:T(8,128)(2,1)S(1)}, bf16[2,96,768]{2,1,0:T(8,128)(2,1)S(1)}, u32[]{:S(2)}, u32[]{:S(2)}) collective-permute-start(bf16[2,96,768]{2,1,0:T(8,128)(2,1)S(1)} %fusion.61), channel_id=1, source_target_pairs={{0,8},{8,0},{16,24},{24,16},{1,9},{9,1},{17,25},{25,17},{2,10},{10... | collective-permute-start | bytes 884744 | tf_op jit(solution)/shard_map/ppermute | solution.py:34
  271.3 9.2 %collective-permute-start.33 = (bf16[96,768]{1,0:T(8,128)(2,1)S(1)}, bf16[96,768]{1,0:T(8,128)(2,1)S(1)}, u32[]{:S(2)}, u32[]{:S(2)}) collective-permute-start(bf16[96,768]{1,0:T(8,128)(2,1)S(1)} %fusion.69), channel_id=1, source_target_pairs={{0,16},{8,24},{16,0},{24,8},{1,17},{9,25},{17,1},{25,9},{2,18},{10... | collective-permute-start | bytes 442376 | tf_op jit(solution)/shard_map/ppermute | solution.py:34
  274.9 8.8 %collective-permute-start.37 = (bf16[96,768]{1,0:T(8,128)(2,1)S(1)}, bf16[96,768]{1,0:T(8,128)(2,1)S(1)}, u32[]{:S(2)}, u32[]{:S(2)}) collective-permute-start(bf16[96,768]{1,0:T(8,128)(2,1)S(1)} %fusion.71), channel_id=1, source_target_pairs={{0,16},{8,24},{16,0},{24,8},{1,17},{9,25},{17,1},{25,9},{2,18},{10... | collective-permute-start | bytes 442376 | tf_op jit(solution)/shard_map/ppermute | solution.py:34
  285.1 35.2 %all-to-all-start = ((bf16[8,96,768]{2,1,0:T(8,128)(2,1)}), bf16[8,96,768]{2,1,0:T(8,128)(2,1)}, u32[]{:S(2)}, u32[]{:S(2)}) async-start(bf16[8,96,768]{2,1,0:T(8,128)(2,1)} %fusion.73), calls=%async_computation | async-start | bytes 2359296 | tf_op jit(solution)/shard_map/all_to_all | solution.py:512
  293.0 15.6 %collective-permute-start.46 = (f32[54,128]{1,0:T(8,128)S(1)}, f32[54,128]{1,0:T(8,128)S(1)}, u32[]{:S(2)}, u32[]{:S(2)}) collective-permute-start(f32[54,128]{1,0:T(8,128)S(1)} %add.430), channel_id=1, source_target_pairs={{0,8},{8,0},{16,24},{24,16},{1,9},{9,1},{17,25},{25,17},{2,10},{10... | collective-permute-start | bytes 82952 | tf_op jit(solution)/shard_map/ppermute | solution.py:34
  295.2 41.4 %collective-permute-start.26 = (bf16[512,768]{1,0:T(8,128)(2,1)S(1)}, bf16[512,768]{1,0:T(8,128)(2,1)}, u32[]{:S(2)}, u32[]{:S(2)}) collective-permute-start(bf16[512,768]{1,0:T(8,128)(2,1)S(1)} %constant_dynamic-slice_fusion.1), channel_id=1, source_target_pairs={{0,2},{2,0},{1,3},{3,1},{4,6},{6,4},{5,7},{7,5},{8,10},{10,8},{9,1... | collective-permute-start | bytes 2359304 | tf_op jit(solution)/shard_map/ppermute | solution.py:34
  318.5 13.2 %collective-permute-start.21 = (bf16[4,96,768]{2,1,0:T(8,128)(2,1)}, bf16[4,96,768]{2,1,0:T(8,128)(2,1)}, u32[]{:S(2)}, u32[]{:S(2)}) collective-permute-start(bf16[4,96,768]{2,1,0:T(8,128)(2,1)} %fusion.49), channel_id=1, source_target_pairs={{0,4},{4,0},{1,5},{5,1},{2,6},{6,2},{3,7},{7,3},{8,12},{12,8},{9,1... | collective-permute-start | bytes 1769480 | tf_op jit(solution)/shard_map/ppermute | solution.py:34
  323.4 22.6 %collective-permute-start.38 = (f32[384,768]{1,0:T(8,128)S(1)}, f32[384,768]{1,0:T(8,128)S(1)}, u32[]{:S(2)}, u32[]{:S(2)}) collective-permute-start(f32[384,768]{1,0:T(8,128)S(1)} %slice_select_fusion), channel_id=1, source_target_pairs={{0,1},{1,0},{2,3},{3,2},{4,5},{5,4},{6,7},{7,6},{8,9},{9,8},{10,11... | collective-permute-start | bytes 3538952 | tf_op jit(solution)/shard_map/ppermute | solution.py:34
  333.1 7.4 %collective-permute-start.28 = (bf16[2,96,768]{2,1,0:T(8,128)(2,1)S(1)}, bf16[2,96,768]{2,1,0:T(8,128)(2,1)S(1)}, u32[]{:S(2)}, u32[]{:S(2)}) collective-permute-start(bf16[2,96,768]{2,1,0:T(8,128)(2,1)S(1)} %fusion.59), channel_id=1, source_target_pairs={{0,8},{8,0},{16,24},{24,16},{1,9},{9,1},{17,25},{25,17},{2,10},{10... | collective-permute-start | bytes 884744 | tf_op jit(solution)/shard_map/ppermute | solution.py:34
  336.5 47.6 %collective-permute-start.27 = (bf16[512,768]{1,0:T(8,128)(2,1)}, bf16[512,768]{1,0:T(8,128)(2,1)}, u32[]{:S(2)}, u32[]{:S(2)}) collective-permute-start(bf16[512,768]{1,0:T(8,128)(2,1)} %collective-permute-done.26), channel_id=1, source_target_pairs={{0,1},{1,0},{2,3},{3,2},{4,5},{5,4},{6,7},{7,6},{8,9},{9,8},{10,11... | collective-permute-start | bytes 2359304 | tf_op jit(solution)/shard_map/ppermute | solution.py:34
  337.6 51.7 %collective-permute-start.22 = (bf16[512,768]{1,0:T(8,128)(2,1)}, bf16[512,768]{1,0:T(8,128)(2,1)}, u32[]{:S(2)}, u32[]{:S(2)}) collective-permute-start(bf16[512,768]{1,0:T(8,128)(2,1)} %constant_dynamic-slice_fusion.2), channel_id=1, source_target_pairs={{0,2},{2,0},{1,3},{3,1},{4,6},{6,4},{5,7},{7,5},{8,10},{10,8},{9,1... | collective-permute-start | bytes 2359304 | tf_op jit(solution)/shard_map/ppermute | solution.py:34
  340.6 9.1 %collective-permute-start.29 = (bf16[96,768]{1,0:T(8,128)(2,1)S(1)}, bf16[96,768]{1,0:T(8,128)(2,1)S(1)}, u32[]{:S(2)}, u32[]{:S(2)}) collective-permute-start(bf16[96,768]{1,0:T(8,128)(2,1)S(1)} %fusion.68), channel_id=1, source_target_pairs={{0,16},{8,24},{16,0},{24,8},{1,17},{9,25},{17,1},{25,9},{2,18},{10... | collective-permute-start | bytes 442376 | tf_op jit(solution)/shard_map/ppermute | solution.py:34
  346.3 36.7 %collective-permute-start.39 = (f32[384,768]{1,0:T(8,128)S(1)}, f32[384,768]{1,0:T(8,128)S(1)}, u32[]{:S(2)}, u32[]{:S(2)}) collective-permute-start(f32[384,768]{1,0:T(8,128)S(1)} %select_add_fusion), channel_id=1, source_target_pairs={{0,2},{2,0},{1,3},{3,1},{4,6},{6,4},{5,7},{7,5},{8,10},{10,8},{9,1... | collective-permute-start | bytes 3538952 | tf_op jit(solution)/shard_map/ppermute | solution.py:34
  354.1 31.6 %all-to-all-start.1 = ((bf16[8,96,192]{2,1,0:T(8,128)(2,1)}), bf16[8,96,192]{2,1,0:T(8,128)(2,1)S(1)}, u32[]{:S(2)}, u32[]{:S(2)}) async-start(bf16[8,96,192]{2,1,0:T(8,128)(2,1)} %fusion.81), calls=%async_computation.1 | async-start | bytes 786432 | tf_op jit(solution)/shard_map/all_to_all | solution.py:512
  384.1 15.1 %collective-permute-start.40 = (f32[384,768]{1,0:T(8,128)}, f32[384,768]{1,0:T(8,128)}, u32[]{:S(2)}, u32[]{:S(2)}) collective-permute-start(f32[384,768]{1,0:T(8,128)} %add.421), channel_id=1, source_target_pairs={{0,1},{1,0},{2,3},{3,2},{4,5},{5,4},{6,7},{7,6},{8,9},{9,8},{10,11... | collective-permute-start | bytes 3538952 | tf_op jit(solution)/shard_map/ppermute | solution.py:34
  385.8 11.6 %collective-permute-start.41 = (bf16[768,192]{1,0:T(8,128)(2,1)S(1)}, bf16[768,192]{1,0:T(8,128)(2,1)S(1)}, u32[]{:S(2)}, u32[]{:S(2)}) collective-permute-start(bf16[768,192]{1,0:T(8,128)(2,1)S(1)} %bitcast.406), channel_id=1, source_target_pairs={{0,2},{2,0},{1,3},{3,1},{4,6},{6,4},{5,7},{7,5},{8,10},{10,8},{9,1... | collective-permute-start | bytes 884744 | tf_op jit(solution)/shard_map/ppermute | solution.py:34
  389.3 92.5 %collective-permute-start.23 = (bf16[512,768]{1,0:T(8,128)(2,1)}, bf16[512,768]{1,0:T(8,128)(2,1)}, u32[]{:S(2)}, u32[]{:S(2)}) collective-permute-start(bf16[512,768]{1,0:T(8,128)(2,1)} %collective-permute-done.22), channel_id=1, source_target_pairs={{0,1},{1,0},{2,3},{3,2},{4,5},{5,4},{6,7},{7,6},{8,9},{9,8},{10,11... | collective-permute-start | bytes 2359304 | tf_op jit(solution)/shard_map/ppermute | solution.py:34
  472.7 35.0 %all-to-all-start.2 = ((bf16[8,96,768]{2,1,0:T(8,128)(2,1)}), bf16[8,96,768]{2,1,0:T(8,128)(2,1)}, u32[]{:S(2)}, u32[]{:S(2)}) async-start(bf16[8,96,768]{2,1,0:T(8,128)(2,1)} %bitcast.398), calls=%async_computation.2 | async-start | bytes 2359296 | tf_op jit(solution)/shard_map/all_to_all | solution.py:525
  (103 other events, 1295.2 us)
